TPU v7x, 512 devices: a whole 4x4x16 slice. The times are simulated.
512 devices in a mesh: sec: 4 (over z_hi, core), gx: 32 (over y, z_lo), gy: 4 (over x).
Axes of the slice: x: 4, y: 4, z: 16 (z_hi: 2, z_lo: 8; z = z_hi * 8 + z_lo), core: 2. Of those that a mesh axis runs over, the one named last changes fastest.
Arguments:
- adjoint: float32 [4, 5, 256, 32, 128], P('sec', None, 'gx', 'gy'), may hold values from -6 to 6
- flow: float32 [4, 6, 256, 32, 128], P('sec', None, 'gx', 'gy'), as said below
- point_cell: int32 [4, 32, 4, 1024], P('sec', 'gx', 'gy'), may hold values from 0 to 8191
- point_dest: int32 [4, 32, 4, 1024], P('sec', 'gx', 'gy'), may hold values from 0 to 127, as said below
- point_target: int32 [4, 32, 4, 1024], P('sec', 'gx', 'gy'), may hold values from 0 to 8191
- point_weight: float32 [4, 32, 4, 1024], P('sec', 'gx', 'gy'), may hold values from 0.5 to 2
- point_count: int32 [4, 32, 4], P('sec', 'gx', 'gy'), may hold values from 0 to 1024, as said below
Outputs:
- adjoint_next: float32 [4, 5, 256, 32, 128], P('sec', None, 'gx', 'gy')
Inputs may be any that keep to these rules, and one draw needn't show every extreme that they name: `flow`: density 0.6 to 1.6, pressure 0.4 (E - kinetic) from 0.5 to 1.5, sponge rate 0.05 to 1. `point_count`: zero on the near-field section; on far-field tiles a multiple of 128, reaching 1024 on some tile. `point_dest`: among the live slots of one far-field tile at most 20 name the same near-field tile, and 20 is reached. Near-field tiles receive unequal numbers of points.
All inputs are finite; a program needn't handle non-finite values.
Results may differ from a plain program's by a relative error of at most 0.00002.
Values sent between devices are 32-bit elements; how exact they have to be, the bound alone decides.
A program may use at most 64 MiB of HBM per device.

v0:
```python
import jax
import jax.numpy as jnp
from jax import lax
from jax.sharding import PartitionSpec as P

GAMMA_MINUS = 0.4
GAMMA_RATIO = 1.4
STEP_SIZE = 0.4


def extended(x, sides, width):
    for axis, dim in sides:
        count, length = (lax.axis_size(axis), x.shape[dim])
        up = [(i, (i + 1) % count) for i in range(count - 1)]
        down = [(j, i) for i, j in up]
        last = lax.slice_in_dim(x, length - width, length, axis=dim)
        initial = lax.slice_in_dim(x, 0, width, axis=dim)
        before = lax.ppermute(last, axis, up)
        after = lax.ppermute(initial, axis, down)
        x = jnp.concatenate([before, x, after], axis=dim)
    return x


def shifted(padded, offset, along):
    length = padded.shape[along] - 6
    return lax.slice_in_dim(padded, 3 + offset, 3 + offset + length, axis=along)


def stencil(padded, along):
    first = shifted(padded, 1, along) - shifted(padded, -1, along)
    second = shifted(padded, 2, along) - shifted(padded, -2, along)
    third = shifted(padded, 3, along) - shifted(padded, -3, along)
    return (45.0 * first - 9.0 * second + third) / 60.0


def wrap_last(values_in):
    return jnp.concatenate([values_in[..., -3:], values_in, values_in[..., :3]], axis=-1)


def fluxes(adjoint, flow, direction):
    density = flow[0]
    inverse = 1.0 / density
    momenta = flow[1:4]
    velocity = momenta[direction] * inverse
    kinetic = (
        0.5
        * (momenta[0] * momenta[0] + momenta[1] * momenta[1] + momenta[2] * momenta[2])
        * inverse
    )
    pressure = GAMMA_MINUS * (flow[4] - kinetic)
    stiffness = GAMMA_RATIO * pressure
    return jnp.stack(
        [
            velocity * adjoint[0],
            velocity * adjoint[1],
            velocity * adjoint[2],
            velocity * adjoint[3],
            velocity * adjoint[4],
            density * adjoint[0] + stiffness * adjoint[4],
            adjoint[1 + direction] * inverse,
        ]
    )


def masked_fluxes(adjoint, flow, direction, inside):
    safe_flow = jnp.concatenate([jnp.where(inside, flow[:1], 1.0), flow[1:]], axis=0)
    return jnp.where(inside, fluxes(adjoint, safe_flow, direction), 0.0)


def assemble(adjoint, flow, along_x, along_y, along_z, source):
    summed = along_x + along_y + along_z
    rate_list = jnp.stack(
        [
            summed[0],
            summed[1] + along_x[5],
            summed[2] + along_y[5],
            summed[3] + along_z[5],
            summed[4] + summed[6],
        ]
    )
    return adjoint + STEP_SIZE * (rate_list - flow[5] * adjoint + source)


def local(adjoint, flow, point_cell, point_dest, point_target, point_weight, point_count):
    adjoint_block = adjoint[0]
    fields = flow[0]
    channels, rows_x, rows_y, depth_cells = adjoint_block.shape
    tile_count = lax.axis_size("gx") * lax.axis_size("gy")
    slot_count = point_cell.shape[-1]
    capacity = 5 * slot_count // (2 * tile_count)
    buffer_width = tile_count * capacity
    cell_index = point_cell.reshape(slot_count)
    dest_tile = point_dest.reshape(slot_count)
    target_cell = point_target.reshape(slot_count)
    flat_block = adjoint_block.reshape(channels, -1)
    values = flat_block[:, cell_index] * point_weight.reshape(slot_count)[None, :]
    live_slot = jnp.arange(slot_count, dtype=jnp.int32) < point_count.reshape(())
    onehot = (
        (dest_tile[:, None] == jnp.arange(tile_count, dtype=jnp.int32)[None, :])
        & live_slot[:, None]
    ).astype(jnp.int32)
    slot_rank = jnp.sum(jnp.cumsum(onehot, axis=0) * onehot, axis=1) - 1
    position = jnp.where(live_slot, dest_tile * capacity + slot_rank, buffer_width)
    packed_values = (
        jnp.zeros((channels, buffer_width), jnp.float32).at[:, position].set(values, mode="drop")
    )
    packed_targets = (
        jnp.zeros((1, buffer_width), jnp.int32).at[0, position].set(target_cell, mode="drop")
    )
    tile_values, tile_targets = (
        lax.all_to_all(packed_values, ("gx", "gy"), split_axis=1, concat_axis=1, tiled=True),
        lax.all_to_all(packed_targets, ("gx", "gy"), split_axis=1, concat_axis=1, tiled=True),
    )
    merged_values, merged_targets = (
        lax.all_gather(tile_values, "sec", axis=1, tiled=True),
        lax.all_gather(tile_targets, "sec", axis=1, tiled=True),
    )
    source = jnp.zeros((channels, rows_x * rows_y * depth_cells), jnp.float32)
    source = (
        source.at[:, merged_targets[0]]
        .add(merged_values)
        .reshape(channels, rows_x, rows_y, depth_cells)
    )
    is_near = lax.axis_index("sec") == lax.axis_size("sec") - 1
    source = jnp.where(is_near, source, 0.0)
    joined = jnp.concatenate([adjoint_block, fields], axis=0)
    padded = extended(joined, (("gx", 1), ("gy", 2)), 3)
    x_position = lax.axis_index("gx") * rows_x - 3 + jnp.arange(rows_x + 6, dtype=jnp.int32)
    x_inside = (x_position >= 0) & (x_position < lax.axis_size("gx") * rows_x)
    y_position = lax.axis_index("gy") * rows_y - 3 + jnp.arange(rows_y + 6, dtype=jnp.int32)
    y_inside = (y_position >= 0) & (y_position < lax.axis_size("gy") * rows_y)
    strip_x = padded[:, :, 3:-3, :]
    flux_x = masked_fluxes(strip_x[:channels], strip_x[channels:], 0, x_inside[:, None, None])
    along_x = stencil(flux_x, 1)
    strip_y = padded[:, 3:-3, :, :]
    flux_y = masked_fluxes(strip_y[:channels], strip_y[channels:], 1, y_inside[None, :, None])
    along_y = stencil(flux_y, 2)
    along_z = stencil(wrap_last(fluxes(adjoint_block, fields, 2)), 3)
    result = assemble(adjoint_block, fields, along_x, along_y, along_z, source)
    return result[None]


def solution(mesh):
    placed = (
        P("sec", None, "gx", "gy", None),
        P("sec", None, "gx", "gy", None),
        P("sec", "gx", "gy", None),
        P("sec", "gx", "gy", None),
        P("sec", "gx", "gy", None),
        P("sec", "gx", "gy", None),
        P("sec", "gx", "gy"),
    )
    return jax.shard_map(
        local,
        mesh=mesh,
        in_specs=placed,
        out_specs=P("sec", None, "gx", "gy", None),
        check_vma=False,
    )
```

profile of v0, /device:TPU:91, one launch (start us, length us, event | category | flops | bytes accessed | tf_op | source)
XLA Modules:
  0.0 205.0 jit_solution(14550307588079525748)
XLA Ops:
  0.0 0.0 copy-start.1
  0.0 0.0 copy-start
  0.0 0.0 copy-start.2
  0.0 0.8 copy.17
  1.5 0.3 fusion.6
  2.0 0.0 copy-start.3
  2.0 0.1 copy.18
  2.1 1.2 fusion.4
  3.3 0.7 compare_select_fusion.2
  4.0 0.8 and_reduce_fusion
  4.8 0.7 fusion.72
  5.6 4.5 %scatter_custom_fusion.2 = s32[2560]{0:T(1024)S(1)} fusion(s32[1024]{0:T(1024)S(1)} %broadcast_select_fusion.3, s32[1024]{0:T(1024)} %bitcast.146, s32[]{:T(128)} %constant.27.clone.1), kind=kCustom, calls=%fused_computation.167 | custom fusion | bytes 10752
  10.0 0.7 all_to_all.16
  10.8 18.3 %all-to-all-start = ((s32[1,128,20]{2,0,1:T(1,128)}), s32[1,128,20]{2,0,1:T(1,128)S(1)}, u32[]{:S(2)}, u32[]{:S(2)}) async-start(s32[1,128,20]{2,0,1:T(1,128)} %bitcast.26), calls=%async_computation | async-start | bytes 131072 | tf_op jit(solution)/shard_map/all_to_all | solution.py:112
  29.1 1.6 pad_maximum_fusion.4
  30.7 2.2 %collective-permute-start.1 = (f32[11,3,8,128]{3,2,1,0:T(8,128)}, f32[11,3,8,128]{3,2,1,0:T(8,128)S(1)}, u32[]{:S(2)}, u32[]{:S(2)}) collective-permute-start(f32[11,3,8,128]{3,2,1,0:T(8,128)} %get-tuple-element.18), channel_id=1, source_target_pairs={{4,0},{8,4},{12,8},{16,12},{20,16},{24,20},{28,24},{32,28},{36,32}... | collective-permute-start | bytes 405512 | tf_op jit(solution)/shard_map/ppermute | solution.py:19
  32.8 3.1 %collective-permute-start = (f32[11,3,8,128]{3,2,1,0:T(8,128)S(1)}, f32[11,3,8,128]{3,2,1,0:T(8,128)S(1)}, u32[]{:S(2)}, u32[]{:S(2)}) collective-permute-start(f32[11,3,8,128]{3,2,1,0:T(8,128)S(1)} %get-tuple-element.17), channel_id=1, source_target_pairs={{0,4},{4,8},{8,12},{12,16},{16,20},{20,24},{24,28},{28,32},{32,36}... | collective-permute-start | bytes 405512 | tf_op jit(solution)/shard_map/ppermute | solution.py:18
  36.0 0.0 copy-done.1
  36.0 0.0 copy-done
  36.0 0.0 copy-done.2
  36.2 0.1 fusion.81
  36.3 2.7 %copy.20 = f32[1,5,8,8,128]{1,4,3,2,0:T(8,128)} copy(f32[1,5,8,8,128]{4,3,2,1,0:T(8,128)S(1)} %copy-done) | data formatting | bytes 327680 | tf_op args[0]
  39.0 0.0 copy-done.3
  39.0 9.7 %scatter_custom_fusion = f32[5,2560]{0,1:T(8,128)S(1)} fusion(s32[1024]{0:T(1024)S(1)} %bitcast.142, f32[]{:T(128)} %constant.32.clone.1, f32[1024]{0:T(1024)S(1)} %bitcast.145, f32[5,8192]{0,1:T(8,128)} %bitcast.136, s32[1024]{0:T(1024)S(1)} %broadcast_clamp_fusion), kind=kCustom, calls=%fused_computation.7 | custom fusion | flops 5120 | bytes 223236 | tf_op jit(solution)/shard_map/scatter | solution.py:105
  48.7 0.4 copy.21
  49.1 0.4 all_to_all.19
  49.5 1.0 copy.22
  50.5 0.0 all-to-all-done
  50.5 23.5 %all-to-all-start.1 = ((f32[5,128,20]{2,0,1:T(8,128)}), f32[5,128,20]{2,0,1:T(8,128)S(1)}, u32[]{:S(2)}, u32[]{:S(2)}) async-start(f32[5,128,20]{2,0,1:T(8,128)} %copy.22), calls=%async_computation.1 | async-start | bytes 1048576 | tf_op jit(solution)/shard_map/all_to_all | solution.py:111
  74.0 0.6 broadcast.293
  74.6 0.8 reduce.7
  75.5 0.1 all_to_all.18
  75.6 27.9 %all_gather.6 = s32[1,10240]{1,0:T(1,128)S(1)} all-gather(s32[1,2560]{1,0:T(1,128)S(1)} %all_to_all.18), channel_id=1, replica_groups=mesh['sec'=4,'gx'=32,'gy'=4] {'sec'}, dimensions={1}, use_global_device_ids=true | all-gather | bytes 51200 | tf_op jit(solution)/shard_map/all_gather | solution.py:116
  103.5 0.0 collective-permute-done.1
  103.5 0.0 collective-permute-done
  103.6 0.9 fusion.80
  104.5 2.2 %collective-permute-start.3 = (f32[11,14,3,128]{3,2,1,0:T(4,128)}, f32[11,14,3,128]{3,2,1,0:T(4,128)S(1)}, u32[]{:S(2)}, u32[]{:S(2)}) collective-permute-start(f32[11,14,3,128]{3,2,1,0:T(4,128)} %get-tuple-element.16), channel_id=1, source_target_pairs={{1,0},{2,1},{3,2},{5,4},{6,5},{7,6},{9,8},{10,9},{11,10},{13,12},{... | collective-permute-start | bytes 709640 | tf_op jit(solution)/shard_map/ppermute | solution.py:19
  106.7 3.3 %collective-permute-start.2 = (f32[11,14,3,128]{3,2,1,0:T(4,128)}, f32[11,14,3,128]{3,2,1,0:T(4,128)S(1)}, u32[]{:S(2)}, u32[]{:S(2)}) collective-permute-start(f32[11,14,3,128]{3,2,1,0:T(4,128)} %get-tuple-element.15), channel_id=1, source_target_pairs={{0,1},{1,2},{2,3},{4,5},{5,6},{6,7},{8,9},{9,10},{10,11},{12,13},{... | collective-permute-start | bytes 709640 | tf_op jit(solution)/shard_map/ppermute | solution.py:18
  110.0 0.1 multiply_dynamic-update-slice_fusion.6
  110.2 0.1 fusion.57
  110.3 0.1 multiply_dynamic-update-slice_fusion.3
  110.4 0.1 broadcast_select_fusion.2
  110.5 0.0 all-to-all-done.1
  110.5 0.1 copy.23
  110.5 0.2 all_to_all.21
  110.8 17.0 %all_gather.7 = f32[5,10240]{1,0:T(8,128)S(1)} all-gather(f32[5,2560]{1,0:T(8,128)S(1)} %all_to_all.21), channel_id=1, replica_groups=mesh['sec'=4,'gx'=32,'gy'=4] {'sec'}, dimensions={1}, use_global_device_ids=true | all-gather | bytes 256000 | tf_op jit(solution)/shard_map/all_gather | solution.py:115
  127.7 3.1 %copy.24 = f32[10240,5]{1,0:T(8,128)} copy(f32[10240,5]{0,1:T(8,128)S(1)} %bitcast.138) | data formatting | bytes 409600 | tf_op jit(solution)/shard_map/all_gather | solution.py:115
  130.9 66.6 %scatter_custom_fusion.1 = f32[5,8192]{0,1:T(8,128)} fusion(s32[10240]{0:T(1024)S(1)} %bitcast.139, f32[10240,5]{1,0:T(8,128)} %copy.24, f32[]{:T(128)} %constant.32.clone.1), kind=kCustom, calls=%fused_computation.5 | custom fusion | flops 51200 | bytes 164352 | tf_op jit(solution)/shard_map/scatter-add | solution.py:121
  197.5 2.3 %broadcast_select_fusion = f32[5,8192]{0,1:T(8,128)} fusion(f32[5,8192]{0,1:T(8,128)} %scatter_custom_fusion.1, pred[]{:T(512)S(6)} %eq.28), kind=kLoop, calls=%fused_computation.4 | loop fusion | flops 40960 | bytes 327681 | tf_op jit(solution)/shard_map/jit(_where)/select_n | solution.py:125
  199.8 2.9 %copy.25 = f32[1,5,8,8,128]{4,3,2,1,0:T(8,128)S(1)} copy(f32[1,5,8,8,128]{1,4,3,2,0:T(8,128)} %bitcast.137) | data formatting | bytes 327680 | tf_op jit(solution)/shard_map/jit(_where)/select_n | solution.py:125
  202.6 0.0 collective-permute-done.3
  202.6 0.0 collective-permute-done.2
  202.7 0.1 multiply_dynamic-update-slice_fusion.2
  202.7 0.1 fusion.49
  202.8 0.1 multiply_dynamic-update-slice_fusion.1
  202.9 0.1 fusion.48
  203.0 0.1 fusion.47
  203.1 0.1 fusion.44
  203.3 0.1 multiply_dynamic-update-slice_fusion
  203.3 0.1 broadcast_select_fusion.1
  203.5 0.7 add_add_fusion
  204.3 0.7 multiply_add_fusion
  (31 shorter events, 0.4 us)
Async XLA Ops:
  0.0 36.0 %copy-start.1 = (f32[1,6,8,8,128]{4,3,2,1,0:T(8,128)S(1)}, f32[1,6,8,8,128]{4,3,2,1,0:T(8,128)}, u32[]{:S(2)}) copy-start(f32[1,6,8,8,128]{4,3,2,1,0:T(8,128)} %param.8) | copy-start | bytes 589828
  0.0 36.0 %copy-start = (f32[1,5,8,8,128]{4,3,2,1,0:T(8,128)S(1)}, f32[1,5,8,8,128]{4,3,2,1,0:T(8,128)}, u32[]{:S(2)}) copy-start(f32[1,5,8,8,128]{4,3,2,1,0:T(8,128)} %param.7) | copy-start | bytes 491524
  0.0 36.0 %copy-start.2 = (s32[1,1,1,1024]{3,2,1,0:T(1,128)S(1)}, s32[1,1,1,1024]{3,2,1,0:T(1,128)}, u32[]{:S(2)}) copy-start(s32[1,1,1,1024]{3,2,1,0:T(1,128)} %param.9) | copy-start | bytes 12292
  2.0 37.0 %copy-start.3 = (f32[1,1,1,1024]{3,2,1,0:T(1,128)S(1)}, f32[1,1,1,1024]{3,2,1,0:T(1,128)}, u32[]{:S(2)}) copy-start(f32[1,1,1,1024]{3,2,1,0:T(1,128)} %param.12) | copy-start | bytes 12292
  10.8 39.7 %all-to-all-start = ((s32[1,128,20]{2,0,1:T(1,128)}), s32[1,128,20]{2,0,1:T(1,128)S(1)}, u32[]{:S(2)}, u32[]{:S(2)}) async-start(s32[1,128,20]{2,0,1:T(1,128)} %bitcast.26), calls=%async_computation | async-start | bytes 131072 | tf_op jit(solution)/shard_map/all_to_all | solution.py:112
  30.7 72.8 %collective-permute-start.1 = (f32[11,3,8,128]{3,2,1,0:T(8,128)}, f32[11,3,8,128]{3,2,1,0:T(8,128)S(1)}, u32[]{:S(2)}, u32[]{:S(2)}) collective-permute-start(f32[11,3,8,128]{3,2,1,0:T(8,128)} %get-tuple-element.18), channel_id=1, source_target_pairs={{4,0},{8,4},{12,8},{16,12},{20,16},{24,20},{28,24},{32,28},{36,32}... | collective-permute-start | bytes 405512 | tf_op jit(solution)/shard_map/ppermute | solution.py:19
  32.8 70.7 %collective-permute-start = (f32[11,3,8,128]{3,2,1,0:T(8,128)S(1)}, f32[11,3,8,128]{3,2,1,0:T(8,128)S(1)}, u32[]{:S(2)}, u32[]{:S(2)}) collective-permute-start(f32[11,3,8,128]{3,2,1,0:T(8,128)S(1)} %get-tuple-element.17), channel_id=1, source_target_pairs={{0,4},{4,8},{8,12},{12,16},{16,20},{20,24},{24,28},{28,32},{32,36}... | collective-permute-start | bytes 405512 | tf_op jit(solution)/shard_map/ppermute | solution.py:18
  50.5 60.0 %all-to-all-start.1 = ((f32[5,128,20]{2,0,1:T(8,128)}), f32[5,128,20]{2,0,1:T(8,128)S(1)}, u32[]{:S(2)}, u32[]{:S(2)}) async-start(f32[5,128,20]{2,0,1:T(8,128)} %copy.22), calls=%async_computation.1 | async-start | bytes 1048576 | tf_op jit(solution)/shard_map/all_to_all | solution.py:111
  104.5 98.1 %collective-permute-start.3 = (f32[11,14,3,128]{3,2,1,0:T(4,128)}, f32[11,14,3,128]{3,2,1,0:T(4,128)S(1)}, u32[]{:S(2)}, u32[]{:S(2)}) collective-permute-start(f32[11,14,3,128]{3,2,1,0:T(4,128)} %get-tuple-element.16), channel_id=1, source_target_pairs={{1,0},{2,1},{3,2},{5,4},{6,5},{7,6},{9,8},{10,9},{11,10},{13,12},{... | collective-permute-start | bytes 709640 | tf_op jit(solution)/shard_map/ppermute | solution.py:19
  106.7 95.9 %collective-permute-start.2 = (f32[11,14,3,128]{3,2,1,0:T(4,128)}, f32[11,14,3,128]{3,2,1,0:T(4,128)S(1)}, u32[]{:S(2)}, u32[]{:S(2)}) collective-permute-start(f32[11,14,3,128]{3,2,1,0:T(4,128)} %get-tuple-element.15), channel_id=1, source_target_pairs={{0,1},{1,2},{2,3},{4,5},{5,6},{6,7},{8,9},{9,10},{10,11},{12,13},{... | collective-permute-start | bytes 709640 | tf_op jit(solution)/shard_map/ppermute | solution.py:18
where the time goes:
time: 206 us; the launch traced here: 205 us
  other arithmetic  87.8 us (43%)
  starting transfers between devices  52.5 us (25%)
  blocking collectives  44.9 us (22%)
  local copies, waits for them, and re-layouts  18.7 us (9%)
    scatter-add x1, other arithmetic, local(): source = source.at[:, merged_targets[0]].add(merged_values).reshape(chann...  66.6 us
    all_gather x1, blocking collectives, local(): lax.all_gather(tile_targets, 'sec', axis=1, tiled=True)  27.9 us
    all_to_all x1, starting transfers between devices, local(): lax.all_to_all(packed_values, ('gx', 'gy'), split_axis=1, concat_axis=1,...  23.5 us
    all_to_all x1, starting transfers between devices, local(): lax.all_to_all(packed_targets, ('gx', 'gy'), split_axis=1, concat_axis=1,...  18.3 us
    all_gather x1, blocking collectives, local(): lax.all_gather(tile_values, 'sec', axis=1, tiled=True)  17 us
    scatter x1, other arithmetic, local(): jnp.zeros((channels, buffer_width), jnp.float32).at[:, position]  9.69 us
    unnamed x11, local copies, waits for them, and re-layouts  7.16 us
    ppermute x2, starting transfers between devices, extended(): before = lax.ppermute(last, axis, up)  6.37 us
  transfers between devices with their start and end apart: 6, of which 0 were waited for; matrix products, arithmetic and copies ran while one was open for 46% of the time, Pallas kernels for 0%

commit v1 on v0

v1 whole, which is shorter than its diff:
```python
import jax
import jax.numpy as jnp
from jax import lax
from jax.experimental import pallas as pl
from jax.experimental.pallas import tpu as pltpu
from jax.sharding import PartitionSpec as P

GAMMA_MINUS = 0.4
GAMMA_RATIO = 1.4
STEP_SIZE = 0.4
FAR = 3
NZ_DEV = 8
NY_DEV = 4
NX_DEV = 4
PLANE = NY_DEV * NX_DEV
SLOTS = 20
F32 = jnp.float32
BF16 = jnp.bfloat16


def iota(shape, dim):
    return lax.broadcasted_iota(jnp.int32, shape, dim)


def two_parts(x):
    high = x.astype(BF16).astype(F32)
    return high, (x - high).astype(BF16).astype(F32)


def onehot(condition):
    return jnp.where(condition, 1.0, 0.0).astype(BF16)


def word_row(word, slot):
    base = 40 * (word // 2)
    return base + slot if word % 2 == 0 else base + 20 + (slot + 4) % 20


def pack(adjoint, cell, dest, target, weight, count):
    points = cell.shape[1]
    live = iota((1, points), 1) < count
    row, lane = cell >> 7, cell & 127
    lanes = onehot(iota((128, points), 0) == lane)
    high, low = two_parts(adjoint)
    parts = jnp.concatenate([high.astype(BF16), low.astype(BF16)], axis=1)
    picked = jnp.dot(
        parts, jnp.concatenate([lanes, lanes], axis=0), preferred_element_type=F32
    )
    row_mask = iota((64, points), 0) == row
    scale = jnp.where(live, weight, 0.0)
    words = [
        jnp.sum(
            jnp.where(row_mask, picked[64 * f : 64 * f + 64], 0.0),
            axis=0,
            keepdims=True,
        )
        * scale
        for f in range(5)
    ]
    words.append(target.astype(F32))
    place = (dest & 96) | ((dest & 3) << 3) | ((dest >> 2) & 7)
    place = jnp.where(live, place, -1)
    tiles = jnp.where(iota((128, points), 0) == place, 1.0, 0.0)
    tiles16 = tiles.astype(BF16)
    before = onehot(iota((256, 256), 0) < iota((256, 256), 1))
    ranks = []
    earlier = jnp.zeros((128, 1), F32)
    for b in range(points // 256):
        block = tiles[:, 256 * b : 256 * b + 256]
        counts = jnp.dot(
            tiles16[:, 256 * b : 256 * b + 256], before, preferred_element_type=F32
        )
        ranks.append(jnp.sum(block * (counts + earlier), axis=0, keepdims=True))
        earlier = earlier + jnp.sum(block, axis=1, keepdims=True)
    rank = jnp.concatenate(ranks, axis=1).astype(jnp.int32)
    eight = iota((8, points), 0)
    first, second, third = eight == rank, eight + 8 == rank, (eight & 3) + 16 == rank
    halves = [two_parts(w) for w in words]
    sides = []
    for side in (0, 1):
        groups = []
        for a, b in ((0, 1), (2, 3), (4, 5)):
            one, two = halves[a][side], halves[b][side]
            groups += [
                jnp.where(first, one, 0.0),
                jnp.where(second, one, 0.0),
                jnp.where(third, jnp.where(eight < 4, one, two), 0.0),
                jnp.where(first, two, 0.0),
                jnp.where(second, two, 0.0),
            ]
        groups.append(jnp.zeros((8, points), F32))
        sides.append(jnp.concatenate(groups, axis=0).astype(BF16))
    packed = lax.dot_general(
        tiles16,
        jnp.concatenate(sides, axis=0),
        (((1,), (1,)), ((), ())),
        preferred_element_type=F32,
    )
    return packed[:, :128] + packed[:, 128:]


def spread(block_ref, lhs_ref, rhs_ref):
    row_iota, lane_iota = iota((32, 128), 0), iota((256, 128), 0)
    for slot in range(SLOTS):
        where = word_row(5, slot)
        target = block_ref[where : where + 1, :].astype(jnp.int32)
        row = (target >> 7) & 31
        lane = (target & 127) | ((target >> 12) << 7)
        row_mask = row_iota == row
        columns = slice(128 * slot, 128 * slot + 128)
        rhs_ref[:, columns] = onehot(lane_iota == lane)
        for f in range(5):
            at = word_row(f, slot)
            high, low = two_parts(block_ref[at : at + 1, :])
            lhs_ref[32 * f : 32 * f + 32, columns] = jnp.where(
                row_mask, high, 0.0
            ).astype(BF16)
            lhs_ref[160 + 32 * f : 192 + 32 * f, columns] = jnp.where(
                row_mask, low, 0.0
            ).astype(BF16)


def differences(at):
    return (
        45.0 * (at(1) - at(-1)) - 9.0 * (at(2) - at(-2)) + (at(3) - at(-3))
    ) * (1.0 / 60.0)


def kernel(
    adjoint_ref,
    flow_ref,
    cell_ref,
    dest_ref,
    target_ref,
    weight_ref,
    count_ref,
    out_ref,
    packed_ref,
    plane_ref,
    near_ref,
    turned_ref,
    lhs_ref,
    rhs_ref,
    x_ref,
    y_ref,
    swap_ref,
    plane_send,
    plane_recv,
    near_send,
    near_recv,
    halo_send,
    halo_recv,
):
    sec, gx, gy = lax.axis_index("sec"), lax.axis_index("gx"), lax.axis_index("gy")
    n_gx, n_gy = lax.axis_size("gx"), lax.axis_size("gy")
    y, z = gx // NZ_DEV, gx % NZ_DEV
    me = y * NX_DEV + gy
    is_far = sec < FAR

    def plane_peer(step):
        q = (me + step) % PLANE
        return q, {"gx": (q // NX_DEV) * NZ_DEV + z, "gy": q % NX_DEV}

    def column(section, z_to):
        return {"sec": section, "gx": y * NZ_DEV + z_to, "gy": gy}

    neighbours = (
        (gx > 0, {"gx": gx - 1}),
        (gx < n_gx - 1, {"gx": gx + 1}),
        (gy > 0, {"gy": gy - 1}),
        (gy < n_gy - 1, {"gy": gy + 1}),
    )

    barrier = pltpu.get_barrier_semaphore()
    expected = jnp.where(is_far, PLANE - 1 + NZ_DEV, 0)
    for exists, device in neighbours:
        expected = expected + jnp.where(exists, 1, 0)

        @pl.when(exists)
        def _(device=device):
            pl.semaphore_signal(barrier, inc=1, device_id=device)

    @pl.when(is_far)
    def _():
        @pl.loop(1, PLANE)
        def _(step):
            pl.semaphore_signal(barrier, inc=1, device_id=plane_peer(step)[1])

    @pl.when(jnp.logical_not(is_far))
    def _():
        @pl.loop(0, FAR * NZ_DEV)
        def _(i):
            pl.semaphore_signal(
                barrier, inc=1, device_id=column(i // NZ_DEV, i % NZ_DEV)
            )

    @pl.when(is_far)
    def _():
        packed_ref[...] = pack(
            adjoint_ref[...],
            cell_ref[...],
            dest_ref[...],
            target_ref[...],
            weight_ref[...],
            count_ref[0, 0],
        )

    pl.semaphore_wait(barrier, expected)

    def own_copy():
        return pltpu.make_async_copy(
            packed_ref.at[pl.ds(pl.multiple_of(me * 8, 8), 8)],
            plane_ref.at[:, me],
            plane_recv,
        )

    def plane_copy(step):
        q, device = plane_peer(step)
        return pltpu.make_async_remote_copy(
            src_ref=packed_ref.at[pl.ds(pl.multiple_of(q * 8, 8), 8)],
            dst_ref=plane_ref.at[:, me],
            send_sem=plane_send,
            recv_sem=plane_recv,
            device_id=device,
        )

    def near_copy(step):
        z_to = (z + step) % NZ_DEV
        return pltpu.make_async_remote_copy(
            src_ref=plane_ref.at[z_to],
            dst_ref=near_ref.at[sec, z],
            send_sem=near_send,
            recv_sem=near_recv.at[sec],
            device_id=column(FAR, z_to),
        )

    @pl.when(is_far)
    def _():
        own_copy().start()

        @pl.loop(1, PLANE)
        def _(step):
            plane_copy(step).start()

    a = [adjoint_ref[64 * f : 64 * f + 64, :] for f in range(5)]
    density, m1, m2, m3, energy, sponge = (
        flow_ref[64 * f : 64 * f + 64, :] for f in range(6)
    )
    inverse = 1.0 / density
    velocity = [m * inverse for m in (m1, m2, m3)]
    kinetic = 0.5 * (m1 * m1 + m2 * m2 + m3 * m3) * inverse
    stiffness = GAMMA_RATIO * (GAMMA_MINUS * (energy - kinetic))
    pressure_like = density * a[0] + stiffness * a[4]

    def flux(direction):
        f = [velocity[direction] * a[i] for i in range(5)]
        f[1 + direction] = f[1 + direction] + pressure_like
        f[4] = f[4] + a[1 + direction] * inverse
        return f

    for f, value in enumerate(flux(0)):
        x_ref[f, 3:11] = value.reshape(8, 8, 128)
    for f, value in enumerate(flux(1)):
        swap_ref[64 * f : 64 * f + 64, :] = value
    for f in range(5):
        for j in range(8):
            y_ref[f, 3 + j] = swap_ref[pl.ds(64 * f + j, 8, stride=8), :]

    halos = []
    for ref, low, high in ((x_ref, 0, 1), (y_ref, 2, 3)):
        halos.append((ref, low, 3, 11, high))
        halos.append((ref, high, 8, 0, low))

    def halo_copy(i):
        ref, side, first, there, _ = halos[i]
        return pltpu.make_async_remote_copy(
            src_ref=ref.at[:, pl.ds(first, 3)],
            dst_ref=ref.at[:, pl.ds(there, 3)],
            send_sem=halo_send.at[i],
            recv_sem=halo_recv.at[i],
            device_id=neighbours[side][1],
        )

    for i in range(4):
        ref, side, _, there, other = halos[i]

        @pl.when(neighbours[side][0])
        def _(i=i):
            halo_copy(i).start()

        @pl.when(jnp.logical_not(neighbours[other][0]))
        def _(ref=ref, there=there):
            ref[:, there : there + 3] = jnp.zeros((5, 3, 8, 128), F32)

    @pl.when(is_far)
    def _():
        pltpu.make_async_copy(plane_ref, plane_ref, plane_recv).wait()

        @pl.loop(0, NZ_DEV)
        def _(step):
            near_copy(step).start()

    flux_z = flux(2)
    rates = []
    for f in range(5):
        value = flux_z[f]
        rates.append(
            differences(lambda o: pltpu.roll(value, (-o) % 128, 1))
        )

    for i in range(4):
        _, side, _, _, other = halos[i]

        @pl.when(neighbours[other][0])
        def _(i=i):
            halo_copy(i).wait_recv()

        @pl.when(neighbours[side][0])
        def _(i=i):
            halo_copy(i).wait_send()

    for f in range(5):
        along_y = differences(lambda o: y_ref[f, 3 + o : 11 + o])
        swap_ref[64 * f : 64 * f + 64, :] = along_y.reshape(64, 128)
    for f in range(5):
        along_x = differences(lambda o: x_ref[f, 3 + o : 11 + o]).reshape(64, 128)
        along_y = jnp.concatenate(
            [swap_ref[pl.ds(64 * f + j, 8, stride=8), :] for j in range(8)], axis=0
        )
        rate = along_x + along_y + rates[f]
        out_ref[64 * f : 64 * f + 64, :] = a[f] + STEP_SIZE * (rate - sponge * a[f])

    @pl.when(jnp.logical_not(is_far))
    def _():
        @pl.loop(0, FAR)
        def _(i):
            section = FAR - 1 - i
            pltpu.make_async_copy(
                near_ref.at[section], near_ref.at[section], near_recv.at[section]
            ).wait()
            turned_ref[...] = near_ref[section].reshape(128, 128).T
            spread(turned_ref, lhs_ref, rhs_ref)
            total = lax.dot_general(
                lhs_ref[...],
                rhs_ref[...],
                (((1,), (1,)), ((), ())),
                preferred_element_type=F32,
            )
            total = STEP_SIZE * (total[:160] + total[160:])
            for f in range(5):
                part = total[32 * f : 32 * f + 32]
                out_ref[64 * f : 64 * f + 32, :] += part[:, :128]
                out_ref[64 * f + 32 : 64 * f + 64, :] += part[:, 128:]

    @pl.when(is_far)
    def _():
        pltpu.make_async_copy(
            packed_ref.at[pl.ds(0, 8 * (PLANE - 1))],
            packed_ref.at[pl.ds(0, 8 * (PLANE - 1))],
            plane_send,
        ).wait()
        pltpu.make_async_copy(plane_ref, plane_ref, near_send).wait()


def local(adjoint, flow, point_cell, point_dest, point_target, point_weight, point_count):
    points = point_cell.shape[-1]
    vmem = pl.BlockSpec(memory_space=pltpu.VMEM)
    out = pl.pallas_call(
        kernel,
        out_shape=jax.ShapeDtypeStruct((320, 128), F32),
        in_specs=[vmem] * 6 + [pl.BlockSpec(memory_space=pltpu.SMEM)],
        out_specs=vmem,
        scratch_shapes=[
            pltpu.VMEM((128, 128), F32),
            pltpu.VMEM((NZ_DEV, PLANE, 128), F32),
            pltpu.VMEM((FAR, NZ_DEV, PLANE, 128), F32),
            pltpu.VMEM((128, 128), F32),
            pltpu.VMEM((320, SLOTS * 128), BF16),
            pltpu.VMEM((256, SLOTS * 128), BF16),
            pltpu.VMEM((5, 14, 8, 128), F32),
            pltpu.VMEM((5, 14, 8, 128), F32),
            pltpu.VMEM((320, 128), F32),
            pltpu.SemaphoreType.DMA,
            pltpu.SemaphoreType.DMA,
            pltpu.SemaphoreType.DMA,
            pltpu.SemaphoreType.DMA((FAR,)),
            pltpu.SemaphoreType.DMA((4,)),
            pltpu.SemaphoreType.DMA((4,)),
        ],
        compiler_params=pltpu.CompilerParams(
            collective_id=0, has_side_effects=True, vmem_limit_bytes=40 * 2**20
        ),
    )(
        adjoint.reshape(320, 128),
        flow.reshape(384, 128),
        point_cell.reshape(1, points),
        point_dest.reshape(1, points),
        point_target.reshape(1, points),
        point_weight.reshape(1, points),
        point_count.reshape(1, 1),
    )
    return out.reshape(1, 5, 8, 8, 128)


def solution(mesh):
    placed = (
        P("sec", None, "gx", "gy", None),
        P("sec", None, "gx", "gy", None),
        P("sec", "gx", "gy", None),
        P("sec", "gx", "gy", None),
        P("sec", "gx", "gy", None),
        P("sec", "gx", "gy", None),
        P("sec", "gx", "gy"),
    )
    return jax.shard_map(
        local,
        mesh=mesh,
        in_specs=placed,
        out_specs=P("sec", None, "gx", "gy", None),
        check_vma=False,
    )
```

time: 206 us -> 31.2 us (0.15)
  the two profiles are of different devices: /device:TPU:91 before, /device:TPU:8 now
where the time goes in v1:
time: 31.2 us; the launch traced here: 30.9 us
  Pallas kernels  26.4 us (85%)
  local copies, waits for them, and re-layouts  3.89 us (12%)
  between operations  0.69 us (2%)
    pallas_call x1, Pallas kernels, local(): pl.pallas_call(kernel, out_shape=jax.ShapeDtypeStruct((320, 128), F32), i...  26.4 us
    unnamed x13, local copies, waits for them, and re-layouts  3.89 us

profile of v1, /device:TPU:8, one launch (start us, length us, event | category | flops | bytes accessed | tf_op | source)
XLA Modules:
  0.0 30.9 jit_solution(2137255094081901406)
XLA Ops:
  0.7 0.0 copy-start.4
  0.7 0.0 copy-start.3
  0.7 0.0 copy-start.2
  0.7 0.7 %copy-done.4 = s32[1,1,1,1024]{3,2,1,0:T(1,128)S(1)} copy-done((s32[1,1,1,1024]{3,2,1,0:T(1,128)S(1)}, s32[1,1,1,1024]{3,2,1,0:T(1,128)}, u32[]{:S(2)}) %copy-start.4) | copy-done | bytes 4120
  1.3 0.0 copy-done.3
  1.4 0.0 copy-done.2
  1.4 0.0 copy-start
  1.4 0.9 %copy-done = f32[1,6,8,8,128]{4,3,2,1,0:T(8,128)S(1)} copy-done((f32[1,6,8,8,128]{4,3,2,1,0:T(8,128)S(1)}, f32[1,6,8,8,128]{4,3,2,1,0:T(8,128)}, u32[]{:S(2)}) %copy-start) | copy-done | bytes 196632
  2.3 0.0 copy-start.1
  2.3 0.9 %copy-done.1 = f32[1,5,8,8,128]{4,3,2,1,0:T(8,128)S(1)} copy-done((f32[1,5,8,8,128]{4,3,2,1,0:T(8,128)S(1)}, f32[1,5,8,8,128]{4,3,2,1,0:T(8,128)}, u32[]{:S(2)}) %copy-start.1) | copy-done | bytes 163864
  3.2 0.0 copy-start.5
  3.2 0.7 %copy-done.5 = f32[1,1,1,1024]{3,2,1,0:T(1,128)S(1)} copy-done((f32[1,1,1,1024]{3,2,1,0:T(1,128)S(1)}, f32[1,1,1,1024]{3,2,1,0:T(1,128)}, u32[]{:S(2)}) %copy-start.5) | copy-done | bytes 4120
  3.9 26.4 %shard_map.73 = f32[320,128]{1,0:T(8,128)S(1)} custom-call(f32[320,128]{1,0:T(8,128)S(1)} %bitcast.11, f32[384,128]{1,0:T(8,128)S(1)} %bitcast.10, s32[1,1024]{1,0:T(1,128)S(1)} %bitcast.12, s32[1,1024]{1,0:T(1,128)S(1)} %bitcast.13, s32[1,1024]{1,0:T(1,128)S(1)} %bitcast.14, f32[1,1024]{1,0:T(1,128)S(1)} %bitcast.15, s32[1,1]{1,0:T(1,128)} %bitcast.8.count_ref), custom_call_target="tpu_custom_call" | custom-call | tf_op jit(solution)/shard_map/pallas_call | solution.py:368
  30.3 0.7 %copy.10 = f32[1,5,8,8,128]{4,3,2,1,0:T(8,128)} copy(f32[1,5,8,8,128]{4,3,2,1,0:T(8,128)S(1)} %bitcast.9) | data formatting | bytes 327680
Async XLA Ops:
  0.7 0.7 %copy-start.4 = (s32[1,1,1,1024]{3,2,1,0:T(1,128)S(1)}, s32[1,1,1,1024]{3,2,1,0:T(1,128)}, u32[]{:S(2)}) copy-start(s32[1,1,1,1024]{3,2,1,0:T(1,128)} %param.11) | copy-start | bytes 12292
  0.7 0.7 %copy-start.3 = (s32[1,1,1,1024]{3,2,1,0:T(1,128)S(1)}, s32[1,1,1,1024]{3,2,1,0:T(1,128)}, u32[]{:S(2)}) copy-start(s32[1,1,1,1024]{3,2,1,0:T(1,128)} %param.10) | copy-start | bytes 12292
  0.7 0.7 %copy-start.2 = (s32[1,1,1,1024]{3,2,1,0:T(1,128)S(1)}, s32[1,1,1,1024]{3,2,1,0:T(1,128)}, u32[]{:S(2)}) copy-start(s32[1,1,1,1024]{3,2,1,0:T(1,128)} %param.9) | copy-start | bytes 12292
  1.4 0.9 %copy-start = (f32[1,6,8,8,128]{4,3,2,1,0:T(8,128)S(1)}, f32[1,6,8,8,128]{4,3,2,1,0:T(8,128)}, u32[]{:S(2)}) copy-start(f32[1,6,8,8,128]{4,3,2,1,0:T(8,128)} %param.8) | copy-start | bytes 589828
  2.3 0.9 %copy-start.1 = (f32[1,5,8,8,128]{4,3,2,1,0:T(8,128)S(1)}, f32[1,5,8,8,128]{4,3,2,1,0:T(8,128)}, u32[]{:S(2)}) copy-start(f32[1,5,8,8,128]{4,3,2,1,0:T(8,128)} %param.7) | copy-start | bytes 491524
  3.2 0.7 %copy-start.5 = (f32[1,1,1,1024]{3,2,1,0:T(1,128)S(1)}, f32[1,1,1,1024]{3,2,1,0:T(1,128)}, u32[]{:S(2)}) copy-start(f32[1,1,1,1024]{3,2,1,0:T(1,128)} %param.12) | copy-start | bytes 12292

commit v2 on v1

--- a/solution.py
+++ b/solution.py
@@ -14,6 +14,7 @@
 NX_DEV = 4
 PLANE = NY_DEV * NX_DEV
 SLOTS = 20
+VMEM_BYTES = 40 * 1024 * 1024
 F32 = jnp.float32
 BF16 = jnp.bfloat16
 
@@ -58,7 +59,7 @@
         for f in range(5)
     ]
     words.append(target.astype(F32))
-    place = (dest & 96) | ((dest & 3) << 3) | ((dest >> 2) & 7)
+    place = ((dest & 3) << 5) | ((dest >> 5) << 3) | ((dest >> 2) & 7)
     place = jnp.where(live, place, -1)
     tiles = jnp.where(iota((128, points), 0) == place, 1.0, 0.0)
     tiles16 = tiles.astype(BF16)
@@ -127,6 +128,14 @@
 
 
 def kernel(
+    adjoint_hbm,
+    flow_hbm,
+    cell_hbm,
+    dest_hbm,
+    target_hbm,
+    weight_hbm,
+    count_hbm,
+    out_ref,
     adjoint_ref,
     flow_ref,
     cell_ref,
@@ -134,9 +143,10 @@
     target_ref,
     weight_ref,
     count_ref,
-    out_ref,
     packed_ref,
-    plane_ref,
+    x_stage_ref,
+    y_stage_ref,
+    column_ref,
     near_ref,
     turned_ref,
     lhs_ref,
@@ -144,55 +154,114 @@
     x_ref,
     y_ref,
     swap_ref,
-    plane_send,
-    plane_recv,
+    in_sem,
+    close_sem,
+    wide_sem,
+    x_send,
+    x_recv,
+    y_send,
+    y_recv,
     near_send,
     near_recv,
     halo_send,
     halo_recv,
 ):
+    loads = [
+        pltpu.make_async_copy(src, dst, in_sem.at[i])
+        for i, (src, dst) in enumerate(
+            (
+                (adjoint_hbm, adjoint_ref),
+                (flow_hbm, flow_ref),
+                (cell_hbm, cell_ref),
+                (dest_hbm, dest_ref),
+                (target_hbm, target_ref),
+                (weight_hbm, weight_ref),
+                (count_hbm, count_ref),
+            )
+        )
+    ]
+    for load in loads:
+        load.start()
+
     sec, gx, gy = lax.axis_index("sec"), lax.axis_index("gx"), lax.axis_index("gy")
     n_gx, n_gy = lax.axis_size("gx"), lax.axis_size("gy")
     y, z = gx // NZ_DEV, gx % NZ_DEV
-    me = y * NX_DEV + gy
     is_far = sec < FAR
-
-    def plane_peer(step):
-        q = (me + step) % PLANE
-        return q, {"gx": (q // NX_DEV) * NZ_DEV + z, "gy": q % NX_DEV}
-
-    def column(section, z_to):
-        return {"sec": section, "gx": y * NZ_DEV + z_to, "gy": gy}
-
+    is_near = sec == FAR
+    core = sec % 2
+    first_core = sec - core
+    low_half = sec < 2
+
+    barrier = pltpu.get_barrier_semaphore()
+
+    def tell(condition, device):
+        @pl.when(condition)
+        def _():
+            pl.semaphore_signal(barrier, inc=1, device_id=device)
+
+    one, zero = jnp.int32(1), jnp.int32(0)
+
+    def number(condition):
+        return jnp.where(condition, one, zero)
+
+    has_low, has_high = gx > 0, gx < n_gx - 1
     neighbours = (
-        (gx > 0, {"gx": gx - 1}),
-        (gx < n_gx - 1, {"gx": gx + 1}),
+        (has_low, {"gx": gx - 1}),
+        (has_high, {"gx": gx + 1}),
         (gy > 0, {"gy": gy - 1}),
         (gy < n_gy - 1, {"gy": gy + 1}),
     )
-
-    barrier = pltpu.get_barrier_semaphore()
-    expected = jnp.where(is_far, PLANE - 1 + NZ_DEV, 0)
-    for exists, device in neighbours:
-        expected = expected + jnp.where(exists, 1, 0)
-
-        @pl.when(exists)
-        def _(device=device):
-            pl.semaphore_signal(barrier, inc=1, device_id=device)
-
-    @pl.when(is_far)
-    def _():
-        @pl.loop(1, PLANE)
-        def _(step):
-            pl.semaphore_signal(barrier, inc=1, device_id=plane_peer(step)[1])
-
-    @pl.when(jnp.logical_not(is_far))
-    def _():
-        @pl.loop(0, FAR * NZ_DEV)
+    tell(has_low, {"sec": first_core, "gx": gx - 1})
+    tell(has_high & (z < NZ_DEV - 1), {"sec": first_core, "gx": gx + 1})
+    tell(has_high & (z == NZ_DEV - 1), {"sec": first_core + 1, "gx": gx + 1})
+    tell(gy > 0, {"sec": first_core, "gy": gy - 1})
+    tell(gy < n_gy - 1, {"sec": first_core, "gy": gy + 1})
+    tell(core == 1, {"sec": first_core})
+    tell(core == 0, {"sec": first_core + 1})
+
+    def x_peer(step):
+        to = (gy + step) % NX_DEV
+        return to, {"gy": to}
+
+    def y_peer(step):
+        to = (y + step) % NY_DEV
+        return to, {"gx": to * NZ_DEV + z}
+
+    @pl.when(is_far)
+    def _():
+        for step in (1, 2, 3):
+            for _, device in (x_peer(step), y_peer(step)):
+                pl.semaphore_signal(
+                    barrier, inc=1, device_id={"sec": first_core, **device}
+                )
+
+    @pl.when(is_near)
+    def _():
+        @pl.loop(0, NZ_DEV)
         def _(i):
-            pl.semaphore_signal(
-                barrier, inc=1, device_id=column(i // NZ_DEV, i % NZ_DEV)
-            )
+            to = {"sec": 1, "gx": y * NZ_DEV + (z + i) % NZ_DEV}
+            pl.semaphore_signal(barrier, inc=1, device_id=to)
+
+        @pl.loop(1, NZ_DEV)
+        def _(i):
+            to = {"gx": y * NZ_DEV + (z + i) % NZ_DEV}
+            pl.semaphore_signal(barrier, inc=1, device_id=to)
+
+    close_count = (
+        2
+        * (
+            number(has_low & (z > 0))
+            + number(has_high)
+            + number(gy > 0)
+            + number(gy < n_gy - 1)
+        )
+        + jnp.where(low_half, 12, 6)
+        + 1
+    )
+    wide_count = jnp.where(low_half, 8, 7) + 2 * number(has_low & (z == 0)) + 1
+
+    for load in loads:
+        load.wait()
 
     @pl.when(is_far)
     def _():
@@ -202,45 +271,8 @@
             dest_ref[...],
             target_ref[...],
             weight_ref[...],
-            count_ref[0, 0],
-        )
-
-    pl.semaphore_wait(barrier, expected)
-
-    def own_copy():
-        return pltpu.make_async_copy(
-            packed_ref.at[pl.ds(pl.multiple_of(me * 8, 8), 8)],
-            plane_ref.at[:, me],
-            plane_recv,
-        )
-
-    def plane_copy(step):
-        q, device = plane_peer(step)
-        return pltpu.make_async_remote_copy(
-            src_ref=packed_ref.at[pl.ds(pl.multiple_of(q * 8, 8), 8)],
-            dst_ref=plane_ref.at[:, me],
-            send_sem=plane_send,
-            recv_sem=plane_recv,
-            device_id=device,
-        )
-
-    def near_copy(step):
-        z_to = (z + step) % NZ_DEV
-        return pltpu.make_async_remote_copy(
-            src_ref=plane_ref.at[z_to],
-            dst_ref=near_ref.at[sec, z],
-            send_sem=near_send,
-            recv_sem=near_recv.at[sec],
-            device_id=column(FAR, z_to),
-        )
-
-    @pl.when(is_far)
-    def _():
-        own_copy().start()
-
-        @pl.loop(1, PLANE)
-        def _(step):
-            plane_copy(step).start()
+            count_ref[0, 0, 0],
+        ).reshape(4, 4, 8, 128)
 
     a = [adjoint_ref[64 * f : 64 * f + 64, :] for f in range(5)]
     density, m1, m2, m3, energy, sponge = (
@@ -265,6 +297,15 @@
     for f in range(5):
         for j in range(8):
             y_ref[f, 3 + j] = swap_ref[pl.ds(64 * f + j, 8, stride=8), :]
+
+    @pl.when(core == 0)
+    def _():
+        pl.semaphore_wait(barrier, close_count)
+        pl.semaphore_signal(close_sem, inc=1, device_id={"sec": first_core + 1})
+
+    @pl.when(core == 1)
+    def _():
+        pl.semaphore_wait(close_sem, 1)
 
     halos = []
     for ref, low, high in ((x_ref, 0, 1), (y_ref, 2, 3)):
@@ -281,10 +322,59 @@
             device_id=neighbours[side][1],
         )
 
-    for i in range(4):
+    def own_x_copy():
+        return pltpu.make_async_copy(
+            packed_ref.at[gy], x_stage_ref.at[gy], x_recv
+        )
+
+    def x_copy(step):
+        to, device = x_peer(step)
+        return pltpu.make_async_remote_copy(
+            src_ref=packed_ref.at[to],
+            dst_ref=x_stage_ref.at[gy],
+            send_sem=x_send,
+            recv_sem=x_recv,
+            device_id=device,
+        )
+
+    def own_y_copy():
+        return pltpu.make_async_copy(
+            x_stage_ref.at[:, y], y_stage_ref.at[y], y_recv
+        )
+
+    def y_copy(step):
+        to, device = y_peer(step)
+        return pltpu.make_async_remote_copy(
+            src_ref=x_stage_ref.at[:, to],
+            dst_ref=y_stage_ref.at[y],
+            send_sem=y_send,
+            recv_sem=y_recv,
+            device_id=device,
+        )
+
+    def near_copy(step):
+        z_to = (z + step) % NZ_DEV
+        return pltpu.make_async_remote_copy(
+            src_ref=column_ref.at[z_to],
+            dst_ref=near_ref.at[sec, z],
+            send_sem=near_send,
+            recv_sem=near_recv.at[sec],
+            device_id={"sec": FAR, "gx": y * NZ_DEV + z_to},
+        )
+
+    @pl.when(is_far)
+    def _():
+        for step in (1, 2, 3):
+            x_copy(step).start()
+        own_x_copy().start()
+
+    for i in (1, 0, 2, 3):
         ref, side, _, there, other = halos[i]
-
-        @pl.when(neighbours[side][0])
+        now = neighbours[side][0]
+        if i == 0:
+            now = now & (z > 0)
+
+        @pl.when(now)
         def _(i=i):
             halo_copy(i).start()
 
@@ -292,45 +382,78 @@
         def _(ref=ref, there=there):
             ref[:, there : there + 3] = jnp.zeros((5, 3, 8, 128), F32)
 
-    @pl.when(is_far)
-    def _():
-        pltpu.make_async_copy(plane_ref, plane_ref, plane_recv).wait()
-
+    flux_z = flux(2)
+    for f in range(5):
+        value = flux_z[f]
+        along_z = differences(lambda o: pltpu.roll(value, (-o) % 128, 1))
+        out_ref[64 * f : 64 * f + 64, :] = a[f] + STEP_SIZE * (along_z - sponge * a[f])
+
+    @pl.when(is_far)
+    def _():
+        pltpu.make_async_copy(x_stage_ref, x_stage_ref, x_recv).wait()
+        for step in (1, 2, 3):
+            y_copy(step).start()
+        own_y_copy().start()
+
+    def add_x(first, last):
+        rows = 8 * (last - first)
+        for f in range(5):
+            along_x = differences(lambda o: x_ref[f, 3 + first + o : 3 + last + o])
+            at = 64 * f + 8 * first
+            out_ref[at : at + rows, :] += STEP_SIZE * along_x.reshape(rows, 128)
+
+    add_x(3, 5)
+
+    @pl.when(is_far)
+    def _():
+        pltpu.make_async_copy(y_stage_ref, y_stage_ref, y_recv).wait()
+        for to in range(NZ_DEV):
+            for x_from in range(NX_DEV):
+                column_ref[to, 4 * x_from : 4 * x_from + 4] = y_stage_ref[
+                    :, x_from, to, :
+                ]
+
+    @pl.when(core == 1)
+    def _():
+        pl.semaphore_wait(barrier, wide_count)
+        pl.semaphore_signal(wide_sem, inc=1, device_id={"sec": first_core})
+
+    @pl.when(core == 0)
+    def _():
+        pl.semaphore_wait(wide_sem, 1)
+
+    @pl.when(has_low & (z == 0))
+    def _():
+        halo_copy(0).start()
+
+    @pl.when(is_far)
+    def _():
         @pl.loop(0, NZ_DEV)
         def _(step):
             near_copy(step).start()
 
-    flux_z = flux(2)
-    rates = []
-    for f in range(5):
-        value = flux_z[f]
-        rates.append(
-            differences(lambda o: pltpu.roll(value, (-o) % 128, 1))
-        )
-
-    for i in range(4):
-        _, side, _, _, other = halos[i]
-
-        @pl.when(neighbours[other][0])
-        def _(i=i):
+    def receive(i):
+        @pl.when(neighbours[halos[i][4]][0])
+        def _():
             halo_copy(i).wait_recv()
 
-        @pl.when(neighbours[side][0])
-        def _(i=i):
-            halo_copy(i).wait_send()
-
+    receive(2)
+    receive(3)
     for f in range(5):
         along_y = differences(lambda o: y_ref[f, 3 + o : 11 + o])
         swap_ref[64 * f : 64 * f + 64, :] = along_y.reshape(64, 128)
     for f in range(5):
-        along_x = differences(lambda o: x_ref[f, 3 + o : 11 + o]).reshape(64, 128)
-        along_y = jnp.concatenate(
-            [swap_ref[pl.ds(64 * f + j, 8, stride=8), :] for j in range(8)], axis=0
-        )
-        rate = along_x + along_y + rates[f]
-        out_ref[64 * f : 64 * f + 64, :] = a[f] + STEP_SIZE * (rate - sponge * a[f])
-
-    @pl.when(jnp.logical_not(is_far))
+        for j in range(8):
+            at = 64 * f + 8 * j
+            out_ref[at : at + 8, :] += (
+                STEP_SIZE * swap_ref[pl.ds(64 * f + j, 8, stride=8), :]
+            )
+    receive(0)
+    add_x(5, 8)
+    receive(1)
+    add_x(0, 3)
+
+    @pl.when(is_near)
     def _():
         @pl.loop(0, FAR)
         def _(i):
@@ -352,26 +475,39 @@
                 out_ref[64 * f : 64 * f + 32, :] += part[:, :128]
                 out_ref[64 * f + 32 : 64 * f + 64, :] += part[:, 128:]
 
-    @pl.when(is_far)
-    def _():
-        pltpu.make_async_copy(
-            packed_ref.at[pl.ds(0, 8 * (PLANE - 1))],
-            packed_ref.at[pl.ds(0, 8 * (PLANE - 1))],
-            plane_send,
-        ).wait()
-        pltpu.make_async_copy(plane_ref, plane_ref, near_send).wait()
+    for i in range(4):
+
+        @pl.when(neighbours[halos[i][1]][0])
+        def _(i=i):
+            halo_copy(i).wait_send()
+
+    @pl.when(is_far)
+    def _():
+        three = packed_ref.at[pl.ds(0, 3)]
+        pltpu.make_async_copy(three, three, x_send).wait()
+        pltpu.make_async_copy(three, three, y_send).wait()
+        pltpu.make_async_copy(column_ref, column_ref, near_send).wait()
 
 
 def local(adjoint, flow, point_cell, point_dest, point_target, point_weight, point_count):
     points = point_cell.shape[-1]
-    vmem = pl.BlockSpec(memory_space=pltpu.VMEM)
+    hbm = pl.BlockSpec(memory_space=pl.ANY)
     out = pl.pallas_call(
         kernel,
         out_shape=jax.ShapeDtypeStruct((320, 128), F32),
-        in_specs=[vmem] * 6 + [pl.BlockSpec(memory_space=pltpu.SMEM)],
-        out_specs=vmem,
+        in_specs=[hbm] * 7,
+        out_specs=pl.BlockSpec(memory_space=pltpu.VMEM),
         scratch_shapes=[
-            pltpu.VMEM((128, 128), F32),
+            pltpu.VMEM((320, 128), F32),
+            pltpu.VMEM((384, 128), F32),
+            pltpu.VMEM((1, points), jnp.int32),
+            pltpu.VMEM((1, points), jnp.int32),
+            pltpu.VMEM((1, points), jnp.int32),
+            pltpu.VMEM((1, points), F32),
+            pltpu.SMEM((1, 1, 1), jnp.int32),
+            pltpu.VMEM((NX_DEV, NY_DEV, NZ_DEV, 128), F32),
+            pltpu.VMEM((NX_DEV, NY_DEV, NZ_DEV, 128), F32),
+            pltpu.VMEM((NY_DEV, NX_DEV, NZ_DEV, 128), F32),
             pltpu.VMEM((NZ_DEV, PLANE, 128), F32),
             pltpu.VMEM((FAR, NZ_DEV, PLANE, 128), F32),
             pltpu.VMEM((128, 128), F32),
@@ -380,6 +516,11 @@
             pltpu.VMEM((5, 14, 8, 128), F32),
             pltpu.VMEM((5, 14, 8, 128), F32),
             pltpu.VMEM((320, 128), F32),
+            pltpu.SemaphoreType.DMA((7,)),
+            pltpu.SemaphoreType.REGULAR,
+            pltpu.SemaphoreType.REGULAR,
+            pltpu.SemaphoreType.DMA,
+            pltpu.SemaphoreType.DMA,
             pltpu.SemaphoreType.DMA,
             pltpu.SemaphoreType.DMA,
             pltpu.SemaphoreType.DMA,
@@ -388,7 +529,7 @@
             pltpu.SemaphoreType.DMA((4,)),
         ],
         compiler_params=pltpu.CompilerParams(
-            collective_id=0, has_side_effects=True, vmem_limit_bytes=40 * 2**20
+            collective_id=0, has_side_effects=True, vmem_limit_bytes=VMEM_BYTES
         ),
     )(
         adjoint.reshape(320, 128),
@@ -397,7 +538,7 @@
         point_dest.reshape(1, points),
         point_target.reshape(1, points),
         point_weight.reshape(1, points),
-        point_count.reshape(1, 1),
+        point_count,
     )
     return out.reshape(1, 5, 8, 8, 128)
 

time: 31.2 us -> 31.1 us (level)
  the two profiles are of different devices: /device:TPU:8 before, /device:TPU:257 now
where the time goes in v2:
time: 31.1 us; the launch traced here: 30.8 us
  Pallas kernels  26.2 us (84%)
  local copies, waits for them, and re-layouts  3.88 us (12%)
  between operations  0.7 us (2%)
    pallas_call x1, Pallas kernels, local(): pl.pallas_call(kernel, out_shape=jax.ShapeDtypeStruct((320, 128), F32), i...  26.2 us
    unnamed x13, local copies, waits for them, and re-layouts  3.88 us

profile of v2, /device:TPU:257, one launch (start us, length us, event | category | flops | bytes accessed | tf_op | source)
XLA Modules:
  0.0 30.8 jit_solution(16666263093253919689)
XLA Ops:
  0.0 0.0 copy-start.4
  0.7 0.0 copy-start.3
  0.7 0.0 copy-start.2
  0.7 0.0 copy-done.4
  0.7 0.7 %copy-done.3 = s32[1,1,1,1024]{3,2,1,0:T(1,128)S(1)} copy-done((s32[1,1,1,1024]{3,2,1,0:T(1,128)S(1)}, s32[1,1,1,1024]{3,2,1,0:T(1,128)}, u32[]{:S(2)}) %copy-start.3) | copy-done | bytes 4120
  1.4 0.0 copy-done.2
  1.4 0.0 copy-start
  1.4 0.9 %copy-done = f32[1,6,8,8,128]{4,3,2,1,0:T(8,128)S(1)} copy-done((f32[1,6,8,8,128]{4,3,2,1,0:T(8,128)S(1)}, f32[1,6,8,8,128]{4,3,2,1,0:T(8,128)}, u32[]{:S(2)}) %copy-start) | copy-done | bytes 196632
  2.3 0.0 copy-start.1
  2.3 0.9 %copy-done.1 = f32[1,5,8,8,128]{4,3,2,1,0:T(8,128)S(1)} copy-done((f32[1,5,8,8,128]{4,3,2,1,0:T(8,128)S(1)}, f32[1,5,8,8,128]{4,3,2,1,0:T(8,128)}, u32[]{:S(2)}) %copy-start.1) | copy-done | bytes 163864
  3.2 0.0 copy-start.5
  3.2 0.7 %copy-done.5 = f32[1,1,1,1024]{3,2,1,0:T(1,128)S(1)} copy-done((f32[1,1,1,1024]{3,2,1,0:T(1,128)S(1)}, f32[1,1,1,1024]{3,2,1,0:T(1,128)}, u32[]{:S(2)}) %copy-start.5) | copy-done | bytes 4120
  3.9 26.2 %shard_map.73 = f32[320,128]{1,0:T(8,128)S(1)} custom-call(f32[320,128]{1,0:T(8,128)S(1)} %bitcast.9, f32[384,128]{1,0:T(8,128)S(1)} %bitcast.8, s32[1,1024]{1,0:T(1,128)S(1)} %bitcast.10, s32[1,1024]{1,0:T(1,128)S(1)} %bitcast.11, s32[1,1024]{1,0:T(1,128)S(1)} %bitcast.12, f32[1,1024]{1,0:T(1,128)S(1)} %bitcast.13, s32[1,1,1]{2,1,0:T(1,128)S(6)} %copy.9.count_hbm), custom_call_target="tpu_custom_call" | custom-call | tf_op jit(solution)/shard_map/pallas_call | solution.py:495
  30.1 0.7 %copy.10 = f32[1,5,8,8,128]{4,3,2,1,0:T(8,128)} copy(f32[1,5,8,8,128]{4,3,2,1,0:T(8,128)S(1)} %bitcast.7) | data formatting | bytes 327680
Async XLA Ops:
  0.0 0.7 %copy-start.4 = (s32[1,1,1,1024]{3,2,1,0:T(1,128)S(1)}, s32[1,1,1,1024]{3,2,1,0:T(1,128)}, u32[]{:S(2)}) copy-start(s32[1,1,1,1024]{3,2,1,0:T(1,128)} %param.11) | copy-start | bytes 12292
  0.7 0.7 %copy-start.3 = (s32[1,1,1,1024]{3,2,1,0:T(1,128)S(1)}, s32[1,1,1,1024]{3,2,1,0:T(1,128)}, u32[]{:S(2)}) copy-start(s32[1,1,1,1024]{3,2,1,0:T(1,128)} %param.10) | copy-start | bytes 12292
  0.7 0.7 %copy-start.2 = (s32[1,1,1,1024]{3,2,1,0:T(1,128)S(1)}, s32[1,1,1,1024]{3,2,1,0:T(1,128)}, u32[]{:S(2)}) copy-start(s32[1,1,1,1024]{3,2,1,0:T(1,128)} %param.9) | copy-start | bytes 12292
  1.4 0.9 %copy-start = (f32[1,6,8,8,128]{4,3,2,1,0:T(8,128)S(1)}, f32[1,6,8,8,128]{4,3,2,1,0:T(8,128)}, u32[]{:S(2)}) copy-start(f32[1,6,8,8,128]{4,3,2,1,0:T(8,128)} %param.8) | copy-start | bytes 589828
  2.3 0.9 %copy-start.1 = (f32[1,5,8,8,128]{4,3,2,1,0:T(8,128)S(1)}, f32[1,5,8,8,128]{4,3,2,1,0:T(8,128)}, u32[]{:S(2)}) copy-start(f32[1,5,8,8,128]{4,3,2,1,0:T(8,128)} %param.7) | copy-start | bytes 491524
  3.2 0.7 %copy-start.5 = (f32[1,1,1,1024]{3,2,1,0:T(1,128)S(1)}, f32[1,1,1,1024]{3,2,1,0:T(1,128)}, u32[]{:S(2)}) copy-start(f32[1,1,1,1024]{3,2,1,0:T(1,128)} %param.12) | copy-start | bytes 12292

commit v3 on v2

--- a/solution.py
+++ b/solution.py
@@ -14,7 +14,7 @@
 NX_DEV = 4
 PLANE = NY_DEV * NX_DEV
 SLOTS = 20
-VMEM_BYTES = 40 * 1024 * 1024
+VMEM_BYTES = 55000 * 1024
 F32 = jnp.float32
 BF16 = jnp.bfloat16
 
@@ -59,7 +59,7 @@
         for f in range(5)
     ]
     words.append(target.astype(F32))
-    place = ((dest & 3) << 5) | ((dest >> 5) << 3) | ((dest >> 2) & 7)
+    place = (dest & 96) | ((dest & 3) << 3) | ((dest >> 2) & 7)
     place = jnp.where(live, place, -1)
     tiles = jnp.where(iota((128, points), 0) == place, 1.0, 0.0)
     tiles16 = tiles.astype(BF16)
@@ -144,8 +144,7 @@
     weight_ref,
     count_ref,
     packed_ref,
-    x_stage_ref,
-    y_stage_ref,
+    plane_ref,
     column_ref,
     near_ref,
     turned_ref,
@@ -155,12 +154,11 @@
     y_ref,
     swap_ref,
     in_sem,
+    turn_sem,
     close_sem,
     wide_sem,
-    x_send,
-    x_recv,
-    y_send,
-    y_recv,
+    plane_send,
+    plane_recv,
     near_send,
     near_recv,
     halo_send,
@@ -191,6 +189,9 @@
     core = sec % 2
     first_core = sec - core
     low_half = sec < 2
+    me = y * NX_DEV + gy
+    last_z = z == NZ_DEV - 1
+    high_turn, low_turn = (gx < n_gx - 1) & last_z, (gx > 0) & (z == 0)
 
     barrier = pltpu.get_barrier_semaphore()
 
@@ -211,68 +212,62 @@
         (gy > 0, {"gy": gy - 1}),
         (gy < n_gy - 1, {"gy": gy + 1}),
     )
-    tell(has_low, {"sec": first_core, "gx": gx - 1})
-    tell(has_high & (z < NZ_DEV - 1), {"sec": first_core, "gx": gx + 1})
-    tell(has_high & (z == NZ_DEV - 1), {"sec": first_core + 1, "gx": gx + 1})
+    tell(has_low & (z > 0), {"sec": first_core, "gx": gx - 1})
+    tell(low_turn, {"sec": first_core + 1, "gx": gx - 1})
+    tell(has_high & jnp.logical_not(last_z), {"sec": first_core, "gx": gx + 1})
+    tell(high_turn, {"sec": first_core + 1, "gx": gx + 1})
     tell(gy > 0, {"sec": first_core, "gy": gy - 1})
     tell(gy < n_gy - 1, {"sec": first_core, "gy": gy + 1})
     tell(core == 1, {"sec": first_core})
     tell(core == 0, {"sec": first_core + 1})
-
-    def x_peer(step):
-        to = (gy + step) % NX_DEV
-        return to, {"gy": to}
-
-    def y_peer(step):
-        to = (y + step) % NY_DEV
-        return to, {"gx": to * NZ_DEV + z}
+    tell(last_z, {"sec": first_core + 1, "gx": gx - 1})
+
+    def plane_peer(step):
+        q = (me + step) % PLANE
+        return q, {"gx": (q // NX_DEV) * NZ_DEV + z, "gy": q % NX_DEV}
 
     @pl.when(is_far)
     def _():
-        for step in (1, 2, 3):
-            for _, device in (x_peer(step), y_peer(step)):
-                pl.semaphore_signal(
-                    barrier, inc=1, device_id={"sec": first_core, **device}
-                )
+        @pl.loop(1, PLANE)
+        def _(step):
+            to = {"sec": first_core, **plane_peer(step)[1]}
+            pl.semaphore_signal(barrier, inc=1, device_id=to)
 
     @pl.when(is_near)
     def _():
-        @pl.loop(0, NZ_DEV)
+        @pl.loop(0, NZ_DEV - 1)
         def _(i):
-            to = {"sec": 1, "gx": y * NZ_DEV + (z + i) % NZ_DEV}
+            to = {"sec": 1, "gx": y * NZ_DEV + i}
             pl.semaphore_signal(barrier, inc=1, device_id=to)
 
-        @pl.loop(1, NZ_DEV)
+        @pl.loop(0, NZ_DEV - 1)
         def _(i):
-            to = {"gx": y * NZ_DEV + (z + i) % NZ_DEV}
-            pl.semaphore_signal(barrier, inc=1, device_id=to)
+            @pl.when(i != z)
+            def _():
+                to = {"gx": y * NZ_DEV + i}
+                pl.semaphore_signal(barrier, inc=1, device_id=to)
 
     close_count = (
         2
         * (
             number(has_low & (z > 0))
-            + number(has_high)
+            + number(has_high & jnp.logical_not(last_z))
             + number(gy > 0)
             + number(gy < n_gy - 1)
         )
-        + jnp.where(low_half, 12, 6)
+        + (PLANE - 1) * jnp.where(low_half, 2, 1)
         + 1
     )
-    wide_count = jnp.where(low_half, 8, 7) + 2 * number(has_low & (z == 0)) + 1
-
-    for load in loads:
-        load.wait()
-
-    @pl.when(is_far)
-    def _():
-        packed_ref[...] = pack(
-            adjoint_ref[...],
-            cell_ref[...],
-            dest_ref[...],
-            target_ref[...],
-            weight_ref[...],
-            count_ref[0, 0, 0],
-        ).reshape(4, 4, 8, 128)
+    wide_count = (
+        jnp.where(low_half, NZ_DEV, NZ_DEV - 1)
+        + 2 * number(low_turn)
+        + 2 * number(z == NZ_DEV - 2)
+        + 1
+    )
+    turn_count = 2 * number(high_turn) + 1
+
+    loads[0].wait()
+    loads[1].wait()
 
     a = [adjoint_ref[64 * f : 64 * f + 64, :] for f in range(5)]
     density, m1, m2, m3, energy, sponge = (
@@ -292,21 +287,6 @@
 
     for f, value in enumerate(flux(0)):
         x_ref[f, 3:11] = value.reshape(8, 8, 128)
-    for f, value in enumerate(flux(1)):
-        swap_ref[64 * f : 64 * f + 64, :] = value
-    for f in range(5):
-        for j in range(8):
-            y_ref[f, 3 + j] = swap_ref[pl.ds(64 * f + j, 8, stride=8), :]
-
-    @pl.when(core == 0)
-    def _():
-        pl.semaphore_wait(barrier, close_count)
-        pl.semaphore_signal(close_sem, inc=1, device_id={"sec": first_core + 1})
-
-    @pl.when(core == 1)
-    def _():
-        pl.semaphore_wait(close_sem, 1)
-
     halos = []
     for ref, low, high in ((x_ref, 0, 1), (y_ref, 2, 3)):
         halos.append((ref, low, 3, 11, high))
@@ -322,57 +302,93 @@
             device_id=neighbours[side][1],
         )
 
-    def own_x_copy():
+    @pl.when(last_z & (core == 1))
+    def _():
+        pl.semaphore_wait(barrier, turn_count)
+        pl.semaphore_signal(turn_sem, inc=1, device_id={"sec": first_core})
+
+    @pl.when(last_z & (core == 0))
+    def _():
+        pl.semaphore_wait(turn_sem, 1)
+
+    @pl.when(high_turn)
+    def _():
+        halo_copy(1).start()
+
+    for load in loads[2:]:
+        load.wait()
+
+    @pl.when(is_far)
+    def _():
+        packed_ref[...] = pack(
+            adjoint_ref[...],
+            cell_ref[...],
+            dest_ref[...],
+            target_ref[...],
+            weight_ref[...],
+            count_ref[0, 0, 0],
+        )
+
+    for f, value in enumerate(flux(1)):
+        swap_ref[64 * f : 64 * f + 64, :] = value
+    for f in range(5):
+        for j in range(8):
+            y_ref[f, 3 + j] = swap_ref[pl.ds(64 * f + j, 8, stride=8), :]
+
+    @pl.when(core == 0)
+    def _():
+        pl.semaphore_wait(barrier, close_count)
+        pl.semaphore_signal(close_sem, inc=1, device_id={"sec": first_core + 1})
+
+    @pl.when(core == 1)
+    def _():
+        pl.semaphore_wait(close_sem, 1)
+
+    def own_copy():
         return pltpu.make_async_copy(
-            packed_ref.at[gy], x_stage_ref.at[gy], x_recv
-        )
-
-    def x_copy(step):
-        to, device = x_peer(step)
+            packed_ref.at[pl.ds(pl.multiple_of(me * 8, 8), 8)],
+            plane_ref.at[me],
+            plane_recv,
+        )
+
+    def plane_copy(step):
+        q, device = plane_peer(step)
         return pltpu.make_async_remote_copy(
-            src_ref=packed_ref.at[to],
-            dst_ref=x_stage_ref.at[gy],
-            send_sem=x_send,
-            recv_sem=x_recv,
+            src_ref=packed_ref.at[pl.ds(pl.multiple_of(q * 8, 8), 8)],
+            dst_ref=plane_ref.at[me],
+            send_sem=plane_send,
+            recv_sem=plane_recv,
             device_id=device,
         )
 
-    def own_y_copy():
-        return pltpu.make_async_copy(
-            x_stage_ref.at[:, y], y_stage_ref.at[y], y_recv
-        )
-
-    def y_copy(step):
-        to, device = y_peer(step)
-        return pltpu.make_async_remote_copy(
-            src_ref=x_stage_ref.at[:, to],
-            dst_ref=y_stage_ref.at[y],
-            send_sem=y_send,
-            recv_sem=y_recv,
-            device_id=device,
-        )
+    chunk = jnp.where(low_half, 1 + z // 4, 0)
+    place = jnp.where(low_half, 4 * core + z % 4, z)
 
     def near_copy(step):
         z_to = (z + step) % NZ_DEV
         return pltpu.make_async_remote_copy(
             src_ref=column_ref.at[z_to],
-            dst_ref=near_ref.at[sec, z],
+            dst_ref=near_ref.at[chunk, place],
             send_sem=near_send,
-            recv_sem=near_recv.at[sec],
+            recv_sem=near_recv.at[chunk],
             device_id={"sec": FAR, "gx": y * NZ_DEV + z_to},
         )
 
     @pl.when(is_far)
     def _():
-        for step in (1, 2, 3):
-            x_copy(step).start()
-        own_x_copy().start()
+        own_copy().start()
+
+        @pl.loop(1, PLANE)
+        def _(step):
+            plane_copy(step).start()
 
     for i in (1, 0, 2, 3):
         ref, side, _, there, other = halos[i]
         now = neighbours[side][0]
         if i == 0:
             now = now & (z > 0)
+        if i == 1:
+            now = now & jnp.logical_not(last_z)
 
         @pl.when(now)
         def _(i=i):
@@ -387,13 +403,6 @@
         value = flux_z[f]
         along_z = differences(lambda o: pltpu.roll(value, (-o) % 128, 1))
         out_ref[64 * f : 64 * f + 64, :] = a[f] + STEP_SIZE * (along_z - sponge * a[f])
-
-    @pl.when(is_far)
-    def _():
-        pltpu.make_async_copy(x_stage_ref, x_stage_ref, x_recv).wait()
-        for step in (1, 2, 3):
-            y_copy(step).start()
-        own_y_copy().start()
 
     def add_x(first, last):
         rows = 8 * (last - first)
@@ -406,23 +415,26 @@
 
     @pl.when(is_far)
     def _():
-        pltpu.make_async_copy(y_stage_ref, y_stage_ref, y_recv).wait()
+        pltpu.make_async_copy(plane_ref, plane_ref, plane_recv).wait()
         for to in range(NZ_DEV):
-            for x_from in range(NX_DEV):
-                column_ref[to, 4 * x_from : 4 * x_from + 4] = y_stage_ref[
-                    :, x_from, to, :
-                ]
-
-    @pl.when(core == 1)
+            column_ref[to] = plane_ref[:, to, :]
+
+    @pl.when((core == 1) & jnp.logical_not(last_z))
     def _():
         pl.semaphore_wait(barrier, wide_count)
         pl.semaphore_signal(wide_sem, inc=1, device_id={"sec": first_core})
 
-    @pl.when(core == 0)
+        @pl.when(z == NZ_DEV - 2)
+        def _():
+            for to in (0, 1):
+                device = {"sec": first_core + to, "gx": gx + 1}
+                pl.semaphore_signal(wide_sem, inc=1, device_id=device)
+
+    @pl.when((core == 0) | last_z)
     def _():
         pl.semaphore_wait(wide_sem, 1)
 
-    @pl.when(has_low & (z == 0))
+    @pl.when(low_turn)
     def _():
         halo_copy(0).start()
 
@@ -457,11 +469,10 @@
     def _():
         @pl.loop(0, FAR)
         def _(i):
-            section = FAR - 1 - i
             pltpu.make_async_copy(
-                near_ref.at[section], near_ref.at[section], near_recv.at[section]
+                near_ref.at[i], near_ref.at[i], near_recv.at[i]
             ).wait()
-            turned_ref[...] = near_ref[section].reshape(128, 128).T
+            turned_ref[...] = near_ref[i].reshape(128, 128).T
             spread(turned_ref, lhs_ref, rhs_ref)
             total = lax.dot_general(
                 lhs_ref[...],
@@ -483,9 +494,8 @@
 
     @pl.when(is_far)
     def _():
-        three = packed_ref.at[pl.ds(0, 3)]
-        pltpu.make_async_copy(three, three, x_send).wait()
-        pltpu.make_async_copy(three, three, y_send).wait()
+        others = packed_ref.at[pl.ds(0, 8 * (PLANE - 1))]
+        pltpu.make_async_copy(others, others, plane_send).wait()
         pltpu.make_async_copy(column_ref, column_ref, near_send).wait()
 
 
@@ -505,9 +515,8 @@
             pltpu.VMEM((1, points), jnp.int32),
             pltpu.VMEM((1, points), F32),
             pltpu.SMEM((1, 1, 1), jnp.int32),
-            pltpu.VMEM((NX_DEV, NY_DEV, NZ_DEV, 128), F32),
-            pltpu.VMEM((NX_DEV, NY_DEV, NZ_DEV, 128), F32),
-            pltpu.VMEM((NY_DEV, NX_DEV, NZ_DEV, 128), F32),
+            pltpu.VMEM((128, 128), F32),
+            pltpu.VMEM((PLANE, NZ_DEV, 128), F32),
             pltpu.VMEM((NZ_DEV, PLANE, 128), F32),
             pltpu.VMEM((FAR, NZ_DEV, PLANE, 128), F32),
             pltpu.VMEM((128, 128), F32),
@@ -519,8 +528,7 @@
             pltpu.SemaphoreType.DMA((7,)),
             pltpu.SemaphoreType.REGULAR,
             pltpu.SemaphoreType.REGULAR,
-            pltpu.SemaphoreType.DMA,
-            pltpu.SemaphoreType.DMA,
+            pltpu.SemaphoreType.REGULAR,
             pltpu.SemaphoreType.DMA,
             pltpu.SemaphoreType.DMA,
             pltpu.SemaphoreType.DMA,
@@ -528,6 +536,9 @@
             pltpu.SemaphoreType.DMA((4,)),
             pltpu.SemaphoreType.DMA((4,)),
         ],
+        cost_estimate=pl.CostEstimate(
+            flops=2 * 10**9, bytes_accessed=10**6, transcendentals=0
+        ),
         compiler_params=pltpu.CompilerParams(
             collective_id=0, has_side_effects=True, vmem_limit_bytes=VMEM_BYTES
         ),

time: 31.1 us -> 27.1 us (0.87)
  Pallas kernels: 26.2 us -> 24.1 us
  local copies, waits for them, and re-layouts: 3.88 us -> 2.04 us
    pallas_call x1, Pallas kernels: 26.2 us -> 24.1 us  [local(): pl.pallas_call(kernel, out_shape=jax.ShapeDtypeStruct((320, 128), F32), i...]
    unnamed x13 -> x9, local copies, waits for them, and re-layouts: 3.88 us -> 2.04 us
where the time goes in v3:
time: 27.1 us; the launch traced here: 26.9 us
  Pallas kernels  24.1 us (89%)
  local copies, waits for them, and re-layouts  2.04 us (8%)
  between operations  0.7 us (3%)
    pallas_call x1, Pallas kernels, local(): pl.pallas_call(kernel, out_shape=jax.ShapeDtypeStruct((320, 128), F32), i...  24.1 us
    unnamed x9, local copies, waits for them, and re-layouts  2.04 us

profile of v3, /device:TPU:257, one launch (start us, length us, event | category | flops | bytes accessed | tf_op | source)
XLA Modules:
  0.0 26.9 jit_solution(12532741054216079163)
XLA Ops:
  0.0 0.0 copy-start.2
  0.7 0.0 copy-start.1
  0.7 0.0 copy-start
  0.7 0.0 copy-done.2
  0.7 0.7 %copy-done.1 = s32[1,1,1,1024]{3,2,1,0:T(1,128)S(1)} copy-done((s32[1,1,1,1024]{3,2,1,0:T(1,128)S(1)}, s32[1,1,1,1024]{3,2,1,0:T(1,128)}, u32[]{:S(2)}) %copy-start.1) | copy-done | bytes 4120
  1.4 0.0 copy-done
  1.4 0.0 copy-start.3
  1.4 0.7 %copy-done.3 = f32[1,1,1,1024]{3,2,1,0:T(1,128)S(1)} copy-done((f32[1,1,1,1024]{3,2,1,0:T(1,128)S(1)}, f32[1,1,1,1024]{3,2,1,0:T(1,128)}, u32[]{:S(2)}) %copy-start.3) | copy-done | bytes 4120
  2.1 24.1 %shard_map.73 = f32[320,128]{1,0:T(8,128)S(1)} custom-call(f32[320,128]{1,0:T(8,128)} %bitcast.13, f32[384,128]{1,0:T(8,128)} %bitcast.12, s32[1,1024]{1,0:T(1,128)S(1)} %bitcast.8, s32[1,1024]{1,0:T(1,128)S(1)} %bitcast.9, s32[1,1024]{1,0:T(1,128)S(1)} %bitcast.10, f32[1,1024]{1,0:T(1,128)S(1)} %bitcast.11, s32[1,1,1]{2,1,0:T(1,128)S(6)} %copy.9.count_hbm), custom_call_target="tpu_custom_call" | custom-call | flops 2000000000 | bytes 1000000 | tf_op jit(solution)/shard_map/pallas_call | solution.py:505
  26.2 0.7 %copy.10 = f32[1,5,8,8,128]{4,3,2,1,0:T(8,128)} copy(f32[1,5,8,8,128]{4,3,2,1,0:T(8,128)S(1)} %bitcast.7) | data formatting | bytes 327680
Async XLA Ops:
  0.0 0.7 %copy-start.2 = (s32[1,1,1,1024]{3,2,1,0:T(1,128)S(1)}, s32[1,1,1,1024]{3,2,1,0:T(1,128)}, u32[]{:S(2)}) copy-start(s32[1,1,1,1024]{3,2,1,0:T(1,128)} %param.11) | copy-start | bytes 12292
  0.7 0.7 %copy-start.1 = (s32[1,1,1,1024]{3,2,1,0:T(1,128)S(1)}, s32[1,1,1,1024]{3,2,1,0:T(1,128)}, u32[]{:S(2)}) copy-start(s32[1,1,1,1024]{3,2,1,0:T(1,128)} %param.10) | copy-start | bytes 12292
  0.7 0.7 %copy-start = (s32[1,1,1,1024]{3,2,1,0:T(1,128)S(1)}, s32[1,1,1,1024]{3,2,1,0:T(1,128)}, u32[]{:S(2)}) copy-start(s32[1,1,1,1024]{3,2,1,0:T(1,128)} %param.9) | copy-start | bytes 12292
  1.4 0.7 %copy-start.3 = (f32[1,1,1,1024]{3,2,1,0:T(1,128)S(1)}, f32[1,1,1,1024]{3,2,1,0:T(1,128)}, u32[]{:S(2)}) copy-start(f32[1,1,1,1024]{3,2,1,0:T(1,128)} %param.12) | copy-start | bytes 12292

commit v4 on v3

--- a/solution.py
+++ b/solution.py
@@ -14,7 +14,7 @@
 NX_DEV = 4
 PLANE = NY_DEV * NX_DEV
 SLOTS = 20
-VMEM_BYTES = 55000 * 1024
+VMEM_BYTES = 40 * 1024 * 1024
 F32 = jnp.float32
 BF16 = jnp.bfloat16
 
@@ -543,12 +543,17 @@
             collective_id=0, has_side_effects=True, vmem_limit_bytes=VMEM_BYTES
         ),
     )(
-        adjoint.reshape(320, 128),
-        flow.reshape(384, 128),
-        point_cell.reshape(1, points),
-        point_dest.reshape(1, points),
-        point_target.reshape(1, points),
-        point_weight.reshape(1, points),
+        *(
+            pltpu.with_memory_space_constraint(v, pltpu.HBM)
+            for v in (
+                adjoint.reshape(320, 128),
+                flow.reshape(384, 128),
+                point_cell.reshape(1, points),
+                point_dest.reshape(1, points),
+                point_target.reshape(1, points),
+                point_weight.reshape(1, points),
+            )
+        ),
         point_count,
     )
     return out.reshape(1, 5, 8, 8, 128)

time: 27.1 us -> 25.6 us (0.945)
  local copies, waits for them, and re-layouts: 2.04 us -> 0.67 us
    unnamed x9 -> x1, local copies, waits for them, and re-layouts: 2.04 us -> 0.67 us
where the time goes in v4:
time: 25.6 us; the launch traced here: 25.4 us
  Pallas kernels  24.1 us (94%)
  local copies, waits for them, and re-layouts  0.67 us (3%)
  between operations  0.66 us (3%)
    pallas_call x1, Pallas kernels, local(): pl.pallas_call(kernel, out_shape=jax.ShapeDtypeStruct((320, 128), F32), i...  24.1 us
    unnamed x1, local copies, waits for them, and re-layouts  0.67 us

profile of v4, /device:TPU:257, one launch (start us, length us, event | category | flops | bytes accessed | tf_op | source)
XLA Modules:
  0.0 25.4 jit_solution(1259123368477574170)
XLA Ops:
  0.7 24.1 %shard_map.73 = f32[320,128]{1,0:T(8,128)S(1)} custom-call(f32[320,128]{1,0:T(8,128)} %bitcast.9, f32[384,128]{1,0:T(8,128)} %bitcast.8, s32[1,1024]{1,0:T(1,128)} %bitcast.10, s32[1,1024]{1,0:T(1,128)} %bitcast.11, s32[1,1024]{1,0:T(1,128)} %bitcast.12, f32[1,1024]{1,0:T(1,128)} %bitcast.13, s32[1,1,1]{2,1,0:T(1,128)S(6)} %copy.9.count_hbm), custom_call_target="tpu_custom_call" | custom-call | flops 2000000000 | bytes 1000000 | tf_op jit(solution)/shard_map/pallas_call | solution.py:505
  24.8 0.7 %copy.10 = f32[1,5,8,8,128]{4,3,2,1,0:T(8,128)} copy(f32[1,5,8,8,128]{4,3,2,1,0:T(8,128)S(1)} %bitcast.7) | data formatting | bytes 327680

commit v5 on v4

--- a/solution.py
+++ b/solution.py
@@ -13,6 +13,10 @@
 NY_DEV = 4
 NX_DEV = 4
 PLANE = NY_DEV * NX_DEV
+STEPS = sorted(
+    ((i, j) for i in range(NY_DEV) for j in range(NX_DEV) if i or j),
+    key=lambda s: -min(s[0], NY_DEV - s[0]) - min(s[1], NX_DEV - s[1]),
+)
 SLOTS = 20
 VMEM_BYTES = 40 * 1024 * 1024
 F32 = jnp.float32
@@ -212,6 +216,34 @@
         (gy > 0, {"gy": gy - 1}),
         (gy < n_gy - 1, {"gy": gy + 1}),
     )
+    def plane_peer(step):
+        to_y, to_x = (y + step[0]) % NY_DEV, (gy + step[1]) % NX_DEV
+        return to_y * NX_DEV + to_x, {"gx": to_y * NZ_DEV + z, "gy": to_x}
+
+    @pl.when(is_near)
+    def _():
+        @pl.loop(0, NZ_DEV)
+        def _(i):
+            z_to = (z + i) % NZ_DEV
+
+            @pl.when(z_to < NZ_DEV - 1)
+            def _():
+                to = {"sec": 1, "gx": y * NZ_DEV + z_to}
+                pl.semaphore_signal(barrier, inc=1, device_id=to)
+
+        @pl.loop(0, NZ_DEV - 1)
+        def _(i):
+            @pl.when(i != z)
+            def _():
+                to = {"gx": y * NZ_DEV + i}
+                pl.semaphore_signal(barrier, inc=1, device_id=to)
+
+    @pl.when(is_far)
+    def _():
+        for step in STEPS:
+            to = {"sec": first_core, **plane_peer(step)[1]}
+            pl.semaphore_signal(barrier, inc=1, device_id=to)
+
     tell(has_low & (z > 0), {"sec": first_core, "gx": gx - 1})
     tell(low_turn, {"sec": first_core + 1, "gx": gx - 1})
     tell(has_high & jnp.logical_not(last_z), {"sec": first_core, "gx": gx + 1})
@@ -222,31 +254,6 @@
     tell(core == 0, {"sec": first_core + 1})
     tell(last_z, {"sec": first_core + 1, "gx": gx - 1})
 
-    def plane_peer(step):
-        q = (me + step) % PLANE
-        return q, {"gx": (q // NX_DEV) * NZ_DEV + z, "gy": q % NX_DEV}
-
-    @pl.when(is_far)
-    def _():
-        @pl.loop(1, PLANE)
-        def _(step):
-            to = {"sec": first_core, **plane_peer(step)[1]}
-            pl.semaphore_signal(barrier, inc=1, device_id=to)
-
-    @pl.when(is_near)
-    def _():
-        @pl.loop(0, NZ_DEV - 1)
-        def _(i):
-            to = {"sec": 1, "gx": y * NZ_DEV + i}
-            pl.semaphore_signal(barrier, inc=1, device_id=to)
-
-        @pl.loop(0, NZ_DEV - 1)
-        def _(i):
-            @pl.when(i != z)
-            def _():
-                to = {"gx": y * NZ_DEV + i}
-                pl.semaphore_signal(barrier, inc=1, device_id=to)
-
     close_count = (
         2
         * (
@@ -365,7 +372,9 @@
     place = jnp.where(low_half, 4 * core + z % 4, z)
 
     def near_copy(step):
-        z_to = (z + step) % NZ_DEV
+        low_to = jnp.where(z < 4, z + step, z - step + NZ_DEV) % NZ_DEV
+        high_to = jnp.where(z < 4, NZ_DEV - 1 - step, step)
+        z_to = jnp.where(low_half, low_to, high_to)
         return pltpu.make_async_remote_copy(
             src_ref=column_ref.at[z_to],
             dst_ref=near_ref.at[chunk, place],
@@ -378,21 +387,22 @@
     def _():
         own_copy().start()
 
-        @pl.loop(1, PLANE)
+        for step in STEPS:
+            plane_copy(step).start()
+
         def _(step):
             plane_copy(step).start()
 
-    for i in (1, 0, 2, 3):
-        ref, side, _, there, other = halos[i]
-        now = neighbours[side][0]
-        if i == 0:
-            now = now & (z > 0)
-        if i == 1:
-            now = now & jnp.logical_not(last_z)
-
-        @pl.when(now)
-        def _(i=i):
+    def start_halo(i, condition):
+        @pl.when(neighbours[halos[i][1]][0] & condition)
+        def _():
             halo_copy(i).start()
+
+    start_halo(1, jnp.logical_not(last_z))
+    start_halo(0, z > 0)
+    start_halo(2, is_near)
+    start_halo(3, is_near)
+    for ref, _, _, there, other in halos:
 
         @pl.when(jnp.logical_not(neighbours[other][0]))
         def _(ref=ref, there=there):
@@ -418,6 +428,9 @@
         pltpu.make_async_copy(plane_ref, plane_ref, plane_recv).wait()
         for to in range(NZ_DEV):
             column_ref[to] = plane_ref[:, to, :]
+
+    start_halo(2, is_far)
+    start_halo(3, is_far)
 
     @pl.when((core == 1) & jnp.logical_not(last_z))
     def _():
@@ -469,10 +482,11 @@
     def _():
         @pl.loop(0, FAR)
         def _(i):
+            k = lax.rem(i + 1, FAR)
             pltpu.make_async_copy(
-                near_ref.at[i], near_ref.at[i], near_recv.at[i]
+                near_ref.at[k], near_ref.at[k], near_recv.at[k]
             ).wait()
-            turned_ref[...] = near_ref[i].reshape(128, 128).T
+            turned_ref[...] = near_ref[k].reshape(128, 128).T
             spread(turned_ref, lhs_ref, rhs_ref)
             total = lax.dot_general(
                 lhs_ref[...],

time: 25.6 us -> 23.2 us (0.906)
  Pallas kernels: 24.1 us -> 21.7 us
    pallas_call x1, Pallas kernels: 24.1 us -> 21.7 us  [local(): pl.pallas_call(kernel, out_shape=jax.ShapeDtypeStruct((320, 128), F32), i...]
where the time goes in v5:
time: 23.2 us; the launch traced here: 23.1 us
  Pallas kernels  21.7 us (94%)
  local copies, waits for them, and re-layouts  0.67 us (3%)
  between operations  0.66 us (3%)
    pallas_call x1, Pallas kernels, local(): pl.pallas_call(kernel, out_shape=jax.ShapeDtypeStruct((320, 128), F32), i...  21.7 us
    unnamed x1, local copies, waits for them, and re-layouts  0.67 us

profile of v5, /device:TPU:257, one launch (start us, length us, event | category | flops | bytes accessed | tf_op | source)
XLA Modules:
  0.0 23.1 jit_solution(10811709461306905461)
XLA Ops:
  0.7 21.7 %shard_map.73 = f32[320,128]{1,0:T(8,128)S(1)} custom-call(f32[320,128]{1,0:T(8,128)} %bitcast.9, f32[384,128]{1,0:T(8,128)} %bitcast.8, s32[1,1024]{1,0:T(1,128)} %bitcast.10, s32[1,1024]{1,0:T(1,128)} %bitcast.11, s32[1,1024]{1,0:T(1,128)} %bitcast.12, f32[1,1024]{1,0:T(1,128)} %bitcast.13, s32[1,1,1]{2,1,0:T(1,128)S(6)} %copy.9.count_hbm), custom_call_target="tpu_custom_call" | custom-call | flops 2000000000 | bytes 1000000 | tf_op jit(solution)/shard_map/pallas_call | solution.py:519
  22.4 0.7 %copy.10 = f32[1,5,8,8,128]{4,3,2,1,0:T(8,128)} copy(f32[1,5,8,8,128]{4,3,2,1,0:T(8,128)S(1)} %bitcast.7) | data formatting | bytes 327680

commit v6 on v5

--- a/solution.py
+++ b/solution.py
@@ -104,16 +104,16 @@
     return packed[:, :128] + packed[:, 128:]
 
 
-def spread(block_ref, lhs_ref, rhs_ref):
-    row_iota, lane_iota = iota((32, 128), 0), iota((256, 128), 0)
+def spread(rows, block_ref, lhs_ref, rhs_ref):
+    row_iota, lane_iota = iota((32, 128), 0), iota((128, 256), 1)
     for slot in range(SLOTS):
         where = word_row(5, slot)
         target = block_ref[where : where + 1, :].astype(jnp.int32)
-        row = (target >> 7) & 31
+        row_mask = row_iota == ((target >> 7) & 31)
+        target = rows[:, where : where + 1].astype(jnp.int32)
         lane = (target & 127) | ((target >> 12) << 7)
-        row_mask = row_iota == row
         columns = slice(128 * slot, 128 * slot + 128)
-        rhs_ref[:, columns] = onehot(lane_iota == lane)
+        rhs_ref[columns, :] = onehot(lane_iota == lane)
         for f in range(5):
             at = word_row(f, slot)
             high, low = two_parts(block_ref[at : at + 1, :])
@@ -160,7 +160,8 @@
     in_sem,
     turn_sem,
     close_sem,
-    wide_sem,
+    lower_sem,
+    upper_sem,
     plane_send,
     plane_recv,
     near_send,
@@ -193,6 +194,7 @@
     core = sec % 2
     first_core = sec - core
     low_half = sec < 2
+    high_half = sec >= 2
     me = y * NX_DEV + gy
     last_z = z == NZ_DEV - 1
     high_turn, low_turn = (gx < n_gx - 1) & last_z, (gx > 0) & (z == 0)
@@ -220,22 +222,30 @@
         to_y, to_x = (y + step[0]) % NY_DEV, (gy + step[1]) % NX_DEV
         return to_y * NX_DEV + to_x, {"gx": to_y * NZ_DEV + z, "gy": to_x}
 
+    tell(low_turn, {"sec": first_core + 1, "gx": gx - 1})
+    tell(high_turn, {"sec": first_core + 1, "gx": gx + jnp.where(low_half, 5, 1)})
+    below = z < 4
+    row = y * NZ_DEV
+
+    @pl.when(is_near & jnp.logical_not(below))
+    def _():
+        for i in range(4):
+            to = {"sec": 1, "gx": row + (z + i) % 4}
+            pl.semaphore_signal(barrier, inc=1, device_id=to)
+
+    @pl.when(is_near & below)
+    def _():
+        for i in range(3):
+            to = {"sec": 1, "gx": row + 4 + i}
+            pl.semaphore_signal(barrier, inc=1, device_id=to)
+
     @pl.when(is_near)
     def _():
-        @pl.loop(0, NZ_DEV)
-        def _(i):
-            z_to = (z + i) % NZ_DEV
-
-            @pl.when(z_to < NZ_DEV - 1)
-            def _():
-                to = {"sec": 1, "gx": y * NZ_DEV + z_to}
-                pl.semaphore_signal(barrier, inc=1, device_id=to)
-
         @pl.loop(0, NZ_DEV - 1)
         def _(i):
             @pl.when(i != z)
             def _():
-                to = {"gx": y * NZ_DEV + i}
+                to = {"gx": row + i}
                 pl.semaphore_signal(barrier, inc=1, device_id=to)
 
     @pl.when(is_far)
@@ -245,9 +255,10 @@
             pl.semaphore_signal(barrier, inc=1, device_id=to)
 
     tell(has_low & (z > 0), {"sec": first_core, "gx": gx - 1})
-    tell(low_turn, {"sec": first_core + 1, "gx": gx - 1})
     tell(has_high & jnp.logical_not(last_z), {"sec": first_core, "gx": gx + 1})
-    tell(high_turn, {"sec": first_core + 1, "gx": gx + 1})
+    tell(low_half & (z < 3), {"sec": first_core + 1, "gx": gx + 4})
+    tell(low_half & (z == 3), {"sec": first_core + 1, "gx": gx + 3})
+    tell(low_half & (z >= 4), {"sec": first_core + 1, "gx": gx - 4})
     tell(gy > 0, {"sec": first_core, "gy": gy - 1})
     tell(gy < n_gy - 1, {"sec": first_core, "gy": gy + 1})
     tell(core == 1, {"sec": first_core})
@@ -265,11 +276,10 @@
         + (PLANE - 1) * jnp.where(low_half, 2, 1)
         + 1
     )
-    wide_count = (
-        jnp.where(low_half, NZ_DEV, NZ_DEV - 1)
-        + 2 * number(low_turn)
-        + 2 * number(z == NZ_DEV - 2)
-        + 1
+    wide_count = jnp.where(
+        low_half,
+        7 + 2 * number((z == 4) & (y > 0)) + 4 * number(z == NZ_DEV - 2),
+        NZ_DEV + 2 * number(low_turn) + 2 * number(z == NZ_DEV - 2),
     )
     turn_count = 2 * number(high_turn) + 1
 
@@ -309,18 +319,21 @@
             device_id=neighbours[side][1],
         )
 
-    @pl.when(last_z & (core == 1))
-    def _():
-        pl.semaphore_wait(barrier, turn_count)
-        pl.semaphore_signal(turn_sem, inc=1, device_id={"sec": first_core})
-
-    @pl.when(last_z & (core == 0))
-    def _():
-        pl.semaphore_wait(turn_sem, 1)
-
-    @pl.when(high_turn)
-    def _():
-        halo_copy(1).start()
+    def turn(half):
+        @pl.when(half & last_z & (core == 1))
+        def _():
+            pl.semaphore_wait(barrier, turn_count)
+            pl.semaphore_signal(turn_sem, inc=1, device_id={"sec": first_core})
+
+        @pl.when(half & last_z & (core == 0))
+        def _():
+            pl.semaphore_wait(turn_sem, 1)
+
+        @pl.when(half & high_turn)
+        def _():
+            halo_copy(1).start()
+
+    turn(low_half)
 
     for load in loads[2:]:
         load.wait()
@@ -371,10 +384,7 @@
     chunk = jnp.where(low_half, 1 + z // 4, 0)
     place = jnp.where(low_half, 4 * core + z % 4, z)
 
-    def near_copy(step):
-        low_to = jnp.where(z < 4, z + step, z - step + NZ_DEV) % NZ_DEV
-        high_to = jnp.where(z < 4, NZ_DEV - 1 - step, step)
-        z_to = jnp.where(low_half, low_to, high_to)
+    def near_copy(z_to):
         return pltpu.make_async_remote_copy(
             src_ref=column_ref.at[z_to],
             dst_ref=near_ref.at[chunk, place],
@@ -386,13 +396,9 @@
     @pl.when(is_far)
     def _():
         own_copy().start()
-
         for step in STEPS:
             plane_copy(step).start()
 
-        def _(step):
-            plane_copy(step).start()
-
     def start_halo(i, condition):
         @pl.when(neighbours[halos[i][1]][0] & condition)
         def _():
@@ -400,8 +406,6 @@
 
     start_halo(1, jnp.logical_not(last_z))
     start_halo(0, z > 0)
-    start_halo(2, is_near)
-    start_halo(3, is_near)
     for ref, _, _, there, other in halos:
 
         @pl.when(jnp.logical_not(neighbours[other][0]))
@@ -423,39 +427,93 @@
 
     add_x(3, 5)
 
+    @pl.when((core == 1) & jnp.logical_not(last_z))
+    def _():
+        pl.semaphore_wait(barrier, wide_count)
+
+        def pass_on(sem, shift):
+            for to in (0, 1):
+                device = {"sec": first_core + to, "gx": gx + shift}
+                pl.semaphore_signal(sem, inc=1, device_id=device)
+
+        @pl.when(low_half & below)
+        def _():
+            pl.semaphore_signal(upper_sem, inc=1, device_id={"sec": first_core})
+            pass_on(upper_sem, 4)
+
+        @pl.when(low_half & jnp.logical_not(below))
+        def _():
+            pl.semaphore_signal(lower_sem, inc=1, device_id={"sec": first_core})
+            pass_on(lower_sem, -4)
+
+        @pl.when(high_half)
+        def _():
+            pl.semaphore_signal(lower_sem, inc=1, device_id={"sec": first_core})
+
+        @pl.when(z == NZ_DEV - 2)
+        def _():
+            pass_on(lower_sem, 1)
+
+        @pl.when(low_half & (z == NZ_DEV - 2))
+        def _():
+            pass_on(lower_sem, -3)
+
+    turn(high_half)
+
+    @pl.when(high_half & ((core == 0) | last_z))
+    def _():
+        pl.semaphore_wait(lower_sem, 1)
+
+    @pl.when(low_turn & jnp.logical_not(low_half))
+    def _():
+        halo_copy(0).start()
+
     @pl.when(is_far)
     def _():
         pltpu.make_async_copy(plane_ref, plane_ref, plane_recv).wait()
         for to in range(NZ_DEV):
             column_ref[to] = plane_ref[:, to, :]
 
-    start_halo(2, is_far)
-    start_halo(3, is_far)
-
-    @pl.when((core == 1) & jnp.logical_not(last_z))
-    def _():
-        pl.semaphore_wait(barrier, wide_count)
-        pl.semaphore_signal(wide_sem, inc=1, device_id={"sec": first_core})
-
-        @pl.when(z == NZ_DEV - 2)
-        def _():
-            for to in (0, 1):
-                device = {"sec": first_core + to, "gx": gx + 1}
-                pl.semaphore_signal(wide_sem, inc=1, device_id=device)
-
-    @pl.when((core == 0) | last_z)
-    def _():
-        pl.semaphore_wait(wide_sem, 1)
-
-    @pl.when(low_turn)
-    def _():
-        halo_copy(0).start()
-
-    @pl.when(is_far)
+    start_halo(2, gy >= 0)
+    start_halo(3, gy >= 0)
+
+    @pl.when(sec == 2)
     def _():
         @pl.loop(0, NZ_DEV)
-        def _(step):
-            near_copy(step).start()
+        def _(j):
+            near_copy(jnp.where(below, NZ_DEV - 1 - j, j)).start()
+
+    def send_four(base, falling):
+        @pl.loop(0, 4)
+        def _(j):
+            near_copy(base + (3 - j if falling else j)).start()
+
+    own = (core == 1) & jnp.logical_not(last_z)
+
+    @pl.when(low_half & below)
+    def _():
+        @pl.when(core == 0)
+        def _():
+            pl.semaphore_wait(upper_sem, 1)
+
+        send_four(4, False)
+        pl.semaphore_wait(lower_sem, 1)
+
+        @pl.when(low_turn)
+        def _():
+            halo_copy(0).start()
+
+        send_four(0, False)
+
+    @pl.when(low_half & jnp.logical_not(below))
+    def _():
+        @pl.when(jnp.logical_not(own))
+        def _():
+            pl.semaphore_wait(lower_sem, 1)
+
+        send_four(0, True)
+        pl.semaphore_wait(upper_sem, 1)
+        send_four(4, True)
 
     def receive(i):
         @pl.when(neighbours[halos[i][4]][0])
@@ -473,32 +531,41 @@
             out_ref[at : at + 8, :] += (
                 STEP_SIZE * swap_ref[pl.ds(64 * f + j, 8, stride=8), :]
             )
-    receive(0)
-    add_x(5, 8)
-    receive(1)
-    add_x(0, 3)
+    def finish_low():
+        receive(1)
+        add_x(0, 3)
+
+    def finish_high():
+        receive(0)
+        add_x(5, 8)
+
+    pl.when(z > 0)(finish_low)
+    pl.when(jnp.logical_not(last_z))(finish_high)
+
+    def add_points(block):
+        rows = block.reshape(128, 128)
+        turned_ref[...] = rows.T
+        spread(rows, turned_ref, lhs_ref, rhs_ref)
+        total = jnp.dot(lhs_ref[...], rhs_ref[...], preferred_element_type=F32)
+        total = STEP_SIZE * (total[:160] + total[160:])
+        for f in range(5):
+            part = total[32 * f : 32 * f + 32]
+            out_ref[64 * f : 64 * f + 32, :] += part[:, :128]
+            out_ref[64 * f + 32 : 64 * f + 64, :] += part[:, 128:]
 
     @pl.when(is_near)
     def _():
         @pl.loop(0, FAR)
         def _(i):
-            k = lax.rem(i + 1, FAR)
+            late = jnp.where(below, 0, 2)
+            k = jnp.where(i == 0, 1, jnp.where(i == 1, 2 - late, late))
             pltpu.make_async_copy(
                 near_ref.at[k], near_ref.at[k], near_recv.at[k]
             ).wait()
-            turned_ref[...] = near_ref[k].reshape(128, 128).T
-            spread(turned_ref, lhs_ref, rhs_ref)
-            total = lax.dot_general(
-                lhs_ref[...],
-                rhs_ref[...],
-                (((1,), (1,)), ((), ())),
-                preferred_element_type=F32,
-            )
-            total = STEP_SIZE * (total[:160] + total[160:])
-            for f in range(5):
-                part = total[32 * f : 32 * f + 32]
-                out_ref[64 * f : 64 * f + 32, :] += part[:, :128]
-                out_ref[64 * f + 32 : 64 * f + 64, :] += part[:, 128:]
+            add_points(near_ref[k])
+
+    pl.when(z == 0)(finish_low)
+    pl.when(last_z)(finish_high)
 
     for i in range(4):
 
@@ -510,6 +577,9 @@
     def _():
         others = packed_ref.at[pl.ds(0, 8 * (PLANE - 1))]
         pltpu.make_async_copy(others, others, plane_send).wait()
+
+    @pl.when(is_far)
+    def _():
         pltpu.make_async_copy(column_ref, column_ref, near_send).wait()
 
 
@@ -535,11 +605,12 @@
             pltpu.VMEM((FAR, NZ_DEV, PLANE, 128), F32),
             pltpu.VMEM((128, 128), F32),
             pltpu.VMEM((320, SLOTS * 128), BF16),
-            pltpu.VMEM((256, SLOTS * 128), BF16),
+            pltpu.VMEM((SLOTS * 128, 256), BF16),
             pltpu.VMEM((5, 14, 8, 128), F32),
             pltpu.VMEM((5, 14, 8, 128), F32),
             pltpu.VMEM((320, 128), F32),
             pltpu.SemaphoreType.DMA((7,)),
+            pltpu.SemaphoreType.REGULAR,
             pltpu.SemaphoreType.REGULAR,
             pltpu.SemaphoreType.REGULAR,
             pltpu.SemaphoreType.REGULAR,

time: 23.2 us -> 22.4 us (0.966)
  the two profiles are of different devices: /device:TPU:257 before, /device:TPU:489 now
where the time goes in v6:
time: 22.4 us; the launch traced here: 22.3 us
  Pallas kernels  21 us (94%)
  local copies, waits for them, and re-layouts  0.67 us (3%)
  between operations  0.66 us (3%)
    pallas_call x1, Pallas kernels, local(): pl.pallas_call(kernel, out_shape=jax.ShapeDtypeStruct((320, 128), F32), i...  21 us
    unnamed x1, local copies, waits for them, and re-layouts  0.67 us

profile of v6, /device:TPU:489, one launch (start us, length us, event | category | flops | bytes accessed | tf_op | source)
XLA Modules:
  0.0 22.3 jit_solution(11319879579485440524)
XLA Ops:
  0.7 21.0 %shard_map.73 = f32[320,128]{1,0:T(8,128)S(1)} custom-call(f32[320,128]{1,0:T(8,128)} %bitcast.9, f32[384,128]{1,0:T(8,128)} %bitcast.8, s32[1,1024]{1,0:T(1,128)} %bitcast.10, s32[1,1024]{1,0:T(1,128)} %bitcast.11, s32[1,1024]{1,0:T(1,128)} %bitcast.12, f32[1,1024]{1,0:T(1,128)} %bitcast.13, s32[1,1,1]{2,1,0:T(1,128)S(6)} %copy.9.count_hbm), custom_call_target="tpu_custom_call" | custom-call | flops 2000000000 | bytes 1000000 | tf_op jit(solution)/shard_map/pallas_call | solution.py:589
  21.6 0.7 %copy.10 = f32[1,5,8,8,128]{4,3,2,1,0:T(8,128)} copy(f32[1,5,8,8,128]{4,3,2,1,0:T(8,128)S(1)} %bitcast.7) | data formatting | bytes 327680

commit v7 on v6

--- a/solution.py
+++ b/solution.py
@@ -511,9 +511,9 @@
         def _():
             pl.semaphore_wait(lower_sem, 1)
 
-        send_four(0, True)
         pl.semaphore_wait(upper_sem, 1)
         send_four(4, True)
+        send_four(0, True)
 
     def receive(i):
         @pl.when(neighbours[halos[i][4]][0])

time: 22.4 us -> 21.6 us (0.964)
  the two profiles are of different devices: /device:TPU:489 before, /device:TPU:425 now
where the time goes in v7:
time: 21.6 us; the launch traced here: 21.5 us
  Pallas kernels  20.2 us (94%)
  local copies, waits for them, and re-layouts  0.67 us (3%)
  between operations  0.66 us (3%)
    pallas_call x1, Pallas kernels, local(): pl.pallas_call(kernel, out_shape=jax.ShapeDtypeStruct((320, 128), F32), i...  20.2 us
    unnamed x1, local copies, waits for them, and re-layouts  0.67 us

profile of v7, /device:TPU:425, one launch (start us, length us, event | category | flops | bytes accessed | tf_op | source)
XLA Modules:
  0.0 21.5 jit_solution(4770584108604933579)
XLA Ops:
  0.7 20.2 %shard_map.73 = f32[320,128]{1,0:T(8,128)S(1)} custom-call(f32[320,128]{1,0:T(8,128)} %bitcast.9, f32[384,128]{1,0:T(8,128)} %bitcast.8, s32[1,1024]{1,0:T(1,128)} %bitcast.10, s32[1,1024]{1,0:T(1,128)} %bitcast.11, s32[1,1024]{1,0:T(1,128)} %bitcast.12, f32[1,1024]{1,0:T(1,128)} %bitcast.13, s32[1,1,1]{2,1,0:T(1,128)S(6)} %copy.9.count_hbm), custom_call_target="tpu_custom_call" | custom-call | flops 2000000000 | bytes 1000000 | tf_op jit(solution)/shard_map/pallas_call | solution.py:589
  20.8 0.7 %copy.10 = f32[1,5,8,8,128]{4,3,2,1,0:T(8,128)} copy(f32[1,5,8,8,128]{4,3,2,1,0:T(8,128)S(1)} %bitcast.7) | data formatting | bytes 327680

commit v8 on v7

--- a/solution.py
+++ b/solution.py
@@ -104,9 +104,9 @@
     return packed[:, :128] + packed[:, 128:]
 
 
-def spread(rows, block_ref, lhs_ref, rhs_ref):
+def spread(slots, rows, block_ref, lhs_ref, rhs_ref):
     row_iota, lane_iota = iota((32, 128), 0), iota((128, 256), 1)
-    for slot in range(SLOTS):
+    for slot in slots:
         where = word_row(5, slot)
         target = block_ref[where : where + 1, :].astype(jnp.int32)
         row_mask = row_iota == ((target >> 7) & 31)
@@ -545,8 +545,14 @@
     def add_points(block):
         rows = block.reshape(128, 128)
         turned_ref[...] = rows.T
-        spread(rows, turned_ref, lhs_ref, rhs_ref)
-        total = jnp.dot(lhs_ref[...], rhs_ref[...], preferred_element_type=F32)
+        total = 0.0
+        for first in (0, SLOTS // 2):
+            slots = range(first, first + SLOTS // 2)
+            spread(slots, rows, turned_ref, lhs_ref, rhs_ref)
+            part = slice(128 * first, 128 * (first + SLOTS // 2))
+            total += jnp.dot(
+                lhs_ref[:, part], rhs_ref[part, :], preferred_element_type=F32
+            )
         total = STEP_SIZE * (total[:160] + total[160:])
         for f in range(5):
             part = total[32 * f : 32 * f + 32]

time: 21.6 us -> 21.6 us (level)
  no operation moved by 1% of the time
where the time goes in v8:
time: 21.6 us; the launch traced here: 21.5 us
  Pallas kernels  20.2 us (94%)
  local copies, waits for them, and re-layouts  0.67 us (3%)
  between operations  0.66 us (3%)
    pallas_call x1, Pallas kernels, local(): pl.pallas_call(kernel, out_shape=jax.ShapeDtypeStruct((320, 128), F32), i...  20.2 us
    unnamed x1, local copies, waits for them, and re-layouts  0.67 us

profile of v8, /device:TPU:425, one launch (start us, length us, event | category | flops | bytes accessed | tf_op | source)
XLA Modules:
  0.0 21.5 jit_solution(17265911364063078190)
XLA Ops:
  0.7 20.2 %shard_map.73 = f32[320,128]{1,0:T(8,128)S(1)} custom-call(f32[320,128]{1,0:T(8,128)} %bitcast.9, f32[384,128]{1,0:T(8,128)} %bitcast.8, s32[1,1024]{1,0:T(1,128)} %bitcast.10, s32[1,1024]{1,0:T(1,128)} %bitcast.11, s32[1,1024]{1,0:T(1,128)} %bitcast.12, f32[1,1024]{1,0:T(1,128)} %bitcast.13, s32[1,1,1]{2,1,0:T(1,128)S(6)} %copy.9.count_hbm), custom_call_target="tpu_custom_call" | custom-call | flops 2000000000 | bytes 1000000 | tf_op jit(solution)/shard_map/pallas_call | solution.py:595
  20.8 0.7 %copy.10 = f32[1,5,8,8,128]{4,3,2,1,0:T(8,128)} copy(f32[1,5,8,8,128]{4,3,2,1,0:T(8,128)S(1)} %bitcast.7) | data formatting | bytes 327680
